TPU v7x, 128 devices: a whole 4x4x4 slice. The times are simulated.
128 devices in a mesh: rows: 8 (over x_lo, y), cols: 16 (over z, x_hi, core).
Axes of the slice: x: 4 (x_hi: 2, x_lo: 2; x = x_hi * 2 + x_lo), y: 4, z: 4, core: 2. Of those that a mesh axis runs over, the one named last changes fastest.
Arguments:
- snapshots: float32 [32768, 2048], P('rows', 'cols'), may hold values from -6 to 6
Outputs:
- rotated: float32 [32768, 2048], P('rows', 'cols')
All inputs are finite; a program needn't handle non-finite values.
Results may differ from a plain program's by a relative error of at most 0.0003.
Values sent between devices are 32-bit elements; how exact they have to be, the bound alone decides.
No kernel may reach another device: no remote copies, remote signals or barrier semaphores. Data moves between devices by JAX's collectives and lax.ppermute only.
A program may use at most 64 MiB of HBM per device.

v0:
```python
import jax
import jax.numpy as jnp
from jax import lax
from jax.sharding import PartitionSpec as P

NS_STEPS = 12


def shifted(block, axis, distance):
    devices = range(lax.axis_size(axis))
    route = [((i - distance) % len(devices), i) for i in devices]
    return lax.ppermute(block, axis, route)


def lowdin(gram):
    size = gram.shape[0]
    diag = jnp.diagonal(gram)
    scale = 1.0 / jnp.sqrt(diag)
    unit = gram * scale[:, None] * scale[None, :]
    eye = jnp.eye(size, dtype=jnp.float32)
    ymat = unit
    zmat = eye
    for step in range(NS_STEPS):
        middle = 1.5 * eye - 0.5 * jnp.dot(zmat, ymat, precision=lax.Precision.HIGHEST)
        ymat = jnp.dot(ymat, middle, precision=lax.Precision.HIGHEST)
        zmat = jnp.dot(middle, zmat, precision=lax.Precision.HIGHEST)
    return scale[:, None] * zmat / scale[None, :]


def inner_rows(left, right):
    return lax.dot_general(
        left,
        right,
        (((0,), (0,)), ((), ())),
        precision=lax.Precision.HIGHEST,
        preferred_element_type=jnp.float32,
    )


def rotate(pair, gram):
    weights = lowdin(gram)
    fresh = jnp.dot(pair, weights, precision=lax.Precision.HIGHEST)
    return (fresh, weights)


def full_gram(top_block, bottom_block):
    pair = jnp.concatenate([top_block, bottom_block], axis=1)
    return (pair, lax.psum(inner_rows(pair, pair), "rows"))


def on_device(snapshots):
    width = snapshots.shape[1] // 2
    top_block = snapshots[:, :width]
    bottom_block = snapshots[:, width:]
    rounds = lax.axis_size("cols") - 1

    def advance(step, state):
        upper, lower = state
        pair, gram = full_gram(upper, lower)
        fresh, weights = rotate(pair, gram)
        lower = shifted(fresh[:, width:], "cols", 1)
        return (fresh[:, :width], lower)

    top_block, bottom_block = lax.fori_loop(0, rounds - 1, advance, (top_block, bottom_block))
    pair, gram = full_gram(top_block, bottom_block)
    fresh, weights = rotate(pair, gram)
    returned = shifted(fresh[:, width:], "cols", 2)
    return jnp.concatenate([fresh[:, :width], returned], axis=1)


def solution(mesh):
    in_specs = (P("rows", "cols"),)
    out_specs = P("rows", "cols")
    return jax.shard_map(
        on_device, mesh=mesh, in_specs=in_specs, out_specs=out_specs, check_vma=False
    )
```

profile of v0, /device:TPU:0, one launch (start us, length us, event | category | flops | bytes accessed | tf_op | source)
XLA Modules:
  0.0 1628.7 jit_solution(803211365654128361)
XLA Ops:
  7.4 4.2 fusion.40
  11.6 2.2 copy.8
  15.3 1491.9 %while.12 = (s32[]{:T(128)}, f32[4096,64]{0,1:T(8,128)S(1)}, f32[4096,64]{0,1:T(8,128)}, s32[]{:T(128)}) while((s32[]{:T(128)}, f32[4096,64]{0,1:T(8,128)S(1)}, f32[4096,64]{0,1:T(8,128)}, s32[]{:T(128)}) %tuple.23), condition=%wide.region_2.3_spmd, body=%wide.region_0.2_spmd.sunk | while | flops 2492350976 | bytes 34542780 | solution.py:64
  16.6 2.4 fusion.403
  19.1 75.4 %all-reduce.5.cloned.1.call-done = f32[128,128]{1,0:T(8,128)} async-done(((f32[128,128]{1,0:T(8,128)}), f32[128,128]{1,0:T(8,128)}) %all-reduce.5.cloned.1.call-update) | async-done | bytes 65552 | tf_op jit(solution)/shard_map/while/body/eval_jaxpr/psum | solution.py:48
  105.6 2.0 fusion.439
  107.8 17.8 %collective-permute-done = f32[4096,64]{0,1:T(8,128)S(1)} collective-permute-done((f32[4096,64]{0,1:T(8,128)S(1)}, f32[4096,64]{0,1:T(8,128)S(1)}, u32[]{:S(2)}, u32[]{:S(2)}) %collective-permute-start) | collective-permute-done | bytes 1048608 | tf_op jit(solution)/shard_map/while/body/eval_jaxpr/ppermute | solution.py:12
  127.9 2.4 fusion.403
  130.4 70.3 %all-reduce.5.cloned.1.call-done = f32[128,128]{1,0:T(8,128)} async-done(((f32[128,128]{1,0:T(8,128)}), f32[128,128]{1,0:T(8,128)}) %all-reduce.5.cloned.1.call-update) | async-done | bytes 65552 | tf_op jit(solution)/shard_map/while/body/eval_jaxpr/psum | solution.py:48
  211.8 2.0 fusion.439
  214.0 17.8 %collective-permute-done = f32[4096,64]{0,1:T(8,128)S(1)} collective-permute-done((f32[4096,64]{0,1:T(8,128)S(1)}, f32[4096,64]{0,1:T(8,128)S(1)}, u32[]{:S(2)}, u32[]{:S(2)}) %collective-permute-start) | collective-permute-done | bytes 1048608 | tf_op jit(solution)/shard_map/while/body/eval_jaxpr/ppermute | solution.py:12
  234.1 2.4 fusion.403
  236.6 70.3 %all-reduce.5.cloned.1.call-done = f32[128,128]{1,0:T(8,128)} async-done(((f32[128,128]{1,0:T(8,128)}), f32[128,128]{1,0:T(8,128)}) %all-reduce.5.cloned.1.call-update) | async-done | bytes 65552 | tf_op jit(solution)/shard_map/while/body/eval_jaxpr/psum | solution.py:48
  318.0 2.0 fusion.439
  320.2 17.8 %collective-permute-done = f32[4096,64]{0,1:T(8,128)S(1)} collective-permute-done((f32[4096,64]{0,1:T(8,128)S(1)}, f32[4096,64]{0,1:T(8,128)S(1)}, u32[]{:S(2)}, u32[]{:S(2)}) %collective-permute-start) | collective-permute-done | bytes 1048608 | tf_op jit(solution)/shard_map/while/body/eval_jaxpr/ppermute | solution.py:12
  340.3 2.4 fusion.403
  342.8 70.3 %all-reduce.5.cloned.1.call-done = f32[128,128]{1,0:T(8,128)} async-done(((f32[128,128]{1,0:T(8,128)}), f32[128,128]{1,0:T(8,128)}) %all-reduce.5.cloned.1.call-update) | async-done | bytes 65552 | tf_op jit(solution)/shard_map/while/body/eval_jaxpr/psum | solution.py:48
  424.2 2.0 fusion.439
  426.4 17.8 %collective-permute-done = f32[4096,64]{0,1:T(8,128)S(1)} collective-permute-done((f32[4096,64]{0,1:T(8,128)S(1)}, f32[4096,64]{0,1:T(8,128)S(1)}, u32[]{:S(2)}, u32[]{:S(2)}) %collective-permute-start) | collective-permute-done | bytes 1048608 | tf_op jit(solution)/shard_map/while/body/eval_jaxpr/ppermute | solution.py:12
  446.5 2.4 fusion.403
  449.0 70.3 %all-reduce.5.cloned.1.call-done = f32[128,128]{1,0:T(8,128)} async-done(((f32[128,128]{1,0:T(8,128)}), f32[128,128]{1,0:T(8,128)}) %all-reduce.5.cloned.1.call-update) | async-done | bytes 65552 | tf_op jit(solution)/shard_map/while/body/eval_jaxpr/psum | solution.py:48
  530.4 2.0 fusion.439
  532.6 17.8 %collective-permute-done = f32[4096,64]{0,1:T(8,128)S(1)} collective-permute-done((f32[4096,64]{0,1:T(8,128)S(1)}, f32[4096,64]{0,1:T(8,128)S(1)}, u32[]{:S(2)}, u32[]{:S(2)}) %collective-permute-start) | collective-permute-done | bytes 1048608 | tf_op jit(solution)/shard_map/while/body/eval_jaxpr/ppermute | solution.py:12
  552.7 2.4 fusion.403
  555.2 70.3 %all-reduce.5.cloned.1.call-done = f32[128,128]{1,0:T(8,128)} async-done(((f32[128,128]{1,0:T(8,128)}), f32[128,128]{1,0:T(8,128)}) %all-reduce.5.cloned.1.call-update) | async-done | bytes 65552 | tf_op jit(solution)/shard_map/while/body/eval_jaxpr/psum | solution.py:48
  636.6 2.0 fusion.439
  638.8 17.8 %collective-permute-done = f32[4096,64]{0,1:T(8,128)S(1)} collective-permute-done((f32[4096,64]{0,1:T(8,128)S(1)}, f32[4096,64]{0,1:T(8,128)S(1)}, u32[]{:S(2)}, u32[]{:S(2)}) %collective-permute-start) | collective-permute-done | bytes 1048608 | tf_op jit(solution)/shard_map/while/body/eval_jaxpr/ppermute | solution.py:12
  658.9 2.4 fusion.403
  661.4 70.3 %all-reduce.5.cloned.1.call-done = f32[128,128]{1,0:T(8,128)} async-done(((f32[128,128]{1,0:T(8,128)}), f32[128,128]{1,0:T(8,128)}) %all-reduce.5.cloned.1.call-update) | async-done | bytes 65552 | tf_op jit(solution)/shard_map/while/body/eval_jaxpr/psum | solution.py:48
  742.8 2.0 fusion.439
  745.0 17.8 %collective-permute-done = f32[4096,64]{0,1:T(8,128)S(1)} collective-permute-done((f32[4096,64]{0,1:T(8,128)S(1)}, f32[4096,64]{0,1:T(8,128)S(1)}, u32[]{:S(2)}, u32[]{:S(2)}) %collective-permute-start) | collective-permute-done | bytes 1048608 | tf_op jit(solution)/shard_map/while/body/eval_jaxpr/ppermute | solution.py:12
  765.1 2.4 fusion.403
  767.6 70.3 %all-reduce.5.cloned.1.call-done = f32[128,128]{1,0:T(8,128)} async-done(((f32[128,128]{1,0:T(8,128)}), f32[128,128]{1,0:T(8,128)}) %all-reduce.5.cloned.1.call-update) | async-done | bytes 65552 | tf_op jit(solution)/shard_map/while/body/eval_jaxpr/psum | solution.py:48
  849.0 2.0 fusion.439
  851.2 17.8 %collective-permute-done = f32[4096,64]{0,1:T(8,128)S(1)} collective-permute-done((f32[4096,64]{0,1:T(8,128)S(1)}, f32[4096,64]{0,1:T(8,128)S(1)}, u32[]{:S(2)}, u32[]{:S(2)}) %collective-permute-start) | collective-permute-done | bytes 1048608 | tf_op jit(solution)/shard_map/while/body/eval_jaxpr/ppermute | solution.py:12
  871.3 2.4 fusion.403
  873.8 70.3 %all-reduce.5.cloned.1.call-done = f32[128,128]{1,0:T(8,128)} async-done(((f32[128,128]{1,0:T(8,128)}), f32[128,128]{1,0:T(8,128)}) %all-reduce.5.cloned.1.call-update) | async-done | bytes 65552 | tf_op jit(solution)/shard_map/while/body/eval_jaxpr/psum | solution.py:48
  955.2 2.0 fusion.439
  957.4 17.8 %collective-permute-done = f32[4096,64]{0,1:T(8,128)S(1)} collective-permute-done((f32[4096,64]{0,1:T(8,128)S(1)}, f32[4096,64]{0,1:T(8,128)S(1)}, u32[]{:S(2)}, u32[]{:S(2)}) %collective-permute-start) | collective-permute-done | bytes 1048608 | tf_op jit(solution)/shard_map/while/body/eval_jaxpr/ppermute | solution.py:12
  977.5 2.4 fusion.403
  980.0 70.3 %all-reduce.5.cloned.1.call-done = f32[128,128]{1,0:T(8,128)} async-done(((f32[128,128]{1,0:T(8,128)}), f32[128,128]{1,0:T(8,128)}) %all-reduce.5.cloned.1.call-update) | async-done | bytes 65552 | tf_op jit(solution)/shard_map/while/body/eval_jaxpr/psum | solution.py:48
  1061.4 2.0 fusion.439
  1063.6 17.8 %collective-permute-done = f32[4096,64]{0,1:T(8,128)S(1)} collective-permute-done((f32[4096,64]{0,1:T(8,128)S(1)}, f32[4096,64]{0,1:T(8,128)S(1)}, u32[]{:S(2)}, u32[]{:S(2)}) %collective-permute-start) | collective-permute-done | bytes 1048608 | tf_op jit(solution)/shard_map/while/body/eval_jaxpr/ppermute | solution.py:12
  1083.7 2.4 fusion.403
  1086.2 70.3 %all-reduce.5.cloned.1.call-done = f32[128,128]{1,0:T(8,128)} async-done(((f32[128,128]{1,0:T(8,128)}), f32[128,128]{1,0:T(8,128)}) %all-reduce.5.cloned.1.call-update) | async-done | bytes 65552 | tf_op jit(solution)/shard_map/while/body/eval_jaxpr/psum | solution.py:48
  1167.6 2.0 fusion.439
  1169.8 17.8 %collective-permute-done = f32[4096,64]{0,1:T(8,128)S(1)} collective-permute-done((f32[4096,64]{0,1:T(8,128)S(1)}, f32[4096,64]{0,1:T(8,128)S(1)}, u32[]{:S(2)}, u32[]{:S(2)}) %collective-permute-start) | collective-permute-done | bytes 1048608 | tf_op jit(solution)/shard_map/while/body/eval_jaxpr/ppermute | solution.py:12
  1189.9 2.4 fusion.403
  1192.4 70.3 %all-reduce.5.cloned.1.call-done = f32[128,128]{1,0:T(8,128)} async-done(((f32[128,128]{1,0:T(8,128)}), f32[128,128]{1,0:T(8,128)}) %all-reduce.5.cloned.1.call-update) | async-done | bytes 65552 | tf_op jit(solution)/shard_map/while/body/eval_jaxpr/psum | solution.py:48
  1273.8 2.0 fusion.439
  1276.0 17.8 %collective-permute-done = f32[4096,64]{0,1:T(8,128)S(1)} collective-permute-done((f32[4096,64]{0,1:T(8,128)S(1)}, f32[4096,64]{0,1:T(8,128)S(1)}, u32[]{:S(2)}, u32[]{:S(2)}) %collective-permute-start) | collective-permute-done | bytes 1048608 | tf_op jit(solution)/shard_map/while/body/eval_jaxpr/ppermute | solution.py:12
  1296.1 2.4 fusion.403
  1298.6 70.3 %all-reduce.5.cloned.1.call-done = f32[128,128]{1,0:T(8,128)} async-done(((f32[128,128]{1,0:T(8,128)}), f32[128,128]{1,0:T(8,128)}) %all-reduce.5.cloned.1.call-update) | async-done | bytes 65552 | tf_op jit(solution)/shard_map/while/body/eval_jaxpr/psum | solution.py:48
  1380.0 2.0 fusion.439
  1382.2 17.8 %collective-permute-done = f32[4096,64]{0,1:T(8,128)S(1)} collective-permute-done((f32[4096,64]{0,1:T(8,128)S(1)}, f32[4096,64]{0,1:T(8,128)S(1)}, u32[]{:S(2)}, u32[]{:S(2)}) %collective-permute-start) | collective-permute-done | bytes 1048608 | tf_op jit(solution)/shard_map/while/body/eval_jaxpr/ppermute | solution.py:12
  1402.3 2.4 fusion.403
  1404.8 70.3 %all-reduce.5.cloned.1.call-done = f32[128,128]{1,0:T(8,128)} async-done(((f32[128,128]{1,0:T(8,128)}), f32[128,128]{1,0:T(8,128)}) %all-reduce.5.cloned.1.call-update) | async-done | bytes 65552 | tf_op jit(solution)/shard_map/while/body/eval_jaxpr/psum | solution.py:48
  1486.2 2.0 fusion.439
  1488.5 17.8 %collective-permute-done = f32[4096,64]{0,1:T(8,128)S(1)} collective-permute-done((f32[4096,64]{0,1:T(8,128)S(1)}, f32[4096,64]{0,1:T(8,128)S(1)}, u32[]{:S(2)}, u32[]{:S(2)}) %collective-permute-start) | collective-permute-done | bytes 1048608 | tf_op jit(solution)/shard_map/while/body/eval_jaxpr/ppermute | solution.py:12
  1509.9 2.4 fusion.63
  1512.3 70.3 %all-reduce.3.cloned.1.call-done = f32[128,128]{1,0:T(8,128)} async-done(((f32[128,128]{1,0:T(8,128)}), f32[128,128]{1,0:T(8,128)}) %all-reduce.3.cloned.1.call-update) | async-done | bytes 65552 | tf_op jit(solution)/shard_map/psum | solution.py:48
  1593.7 2.0 fusion.84
  1595.9 2.8 collective-permute-start.1
  1598.7 21.0 %collective-permute-done.1 = f32[4096,64]{0,1:T(8,128)S(1)} collective-permute-done((f32[4096,64]{0,1:T(8,128)S(1)}, f32[4096,64]{0,1:T(8,128)S(1)}, u32[]{:S(2)}, u32[]{:S(2)}) %collective-permute-start.1) | collective-permute-done | bytes 1048608 | tf_op jit(solution)/shard_map/ppermute | solution.py:12
  (724 shorter events, 204.2 us)
Async XLA Ops:
  15.3 79.1 %all-reduce.5.cloned.1.call-start = ((), (), s32[]{:S(2)}) async-start(), calls=%async_computation.1 | async-start | bytes 131072 | tf_op jit(solution)/shard_map/while/body/eval_jaxpr/psum | solution.py:48
  15.3 1.2 copy-start
  107.7 17.9 %collective-permute-start = (f32[4096,64]{0,1:T(8,128)S(1)}, f32[4096,64]{0,1:T(8,128)S(1)}, u32[]{:S(2)}, u32[]{:S(2)}) collective-permute-start(f32[4096,64]{0,1:T(8,128)S(1)} %get-tuple-element.59), channel_id=1, source_target_pairs={{15,0},{0,1},{1,2},{2,3},{3,4},{4,5},{5,6},{6,7},{7,8},{8,9},{9,10... | collective-permute-start | bytes 3145736 | tf_op jit(solution)/shard_map/while/body/eval_jaxpr/ppermute | solution.py:12
  125.6 1.0 copy-start.1
  126.6 74.0 %all-reduce.5.cloned.1.call-start = ((), (), s32[]{:S(2)}) async-start(), calls=%async_computation.1 | async-start | bytes 131072 | tf_op jit(solution)/shard_map/while/body/eval_jaxpr/psum | solution.py:48
  126.6 1.2 copy-start
  213.9 17.9 %collective-permute-start = (f32[4096,64]{0,1:T(8,128)S(1)}, f32[4096,64]{0,1:T(8,128)S(1)}, u32[]{:S(2)}, u32[]{:S(2)}) collective-permute-start(f32[4096,64]{0,1:T(8,128)S(1)} %get-tuple-element.59), channel_id=1, source_target_pairs={{15,0},{0,1},{1,2},{2,3},{3,4},{4,5},{5,6},{6,7},{7,8},{8,9},{9,10... | collective-permute-start | bytes 3145736 | tf_op jit(solution)/shard_map/while/body/eval_jaxpr/ppermute | solution.py:12
  231.8 1.0 copy-start.1
  232.8 74.0 %all-reduce.5.cloned.1.call-start = ((), (), s32[]{:S(2)}) async-start(), calls=%async_computation.1 | async-start | bytes 131072 | tf_op jit(solution)/shard_map/while/body/eval_jaxpr/psum | solution.py:48
  232.8 1.2 copy-start
  320.1 17.9 %collective-permute-start = (f32[4096,64]{0,1:T(8,128)S(1)}, f32[4096,64]{0,1:T(8,128)S(1)}, u32[]{:S(2)}, u32[]{:S(2)}) collective-permute-start(f32[4096,64]{0,1:T(8,128)S(1)} %get-tuple-element.59), channel_id=1, source_target_pairs={{15,0},{0,1},{1,2},{2,3},{3,4},{4,5},{5,6},{6,7},{7,8},{8,9},{9,10... | collective-permute-start | bytes 3145736 | tf_op jit(solution)/shard_map/while/body/eval_jaxpr/ppermute | solution.py:12
  338.0 1.0 copy-start.1
  339.0 74.0 %all-reduce.5.cloned.1.call-start = ((), (), s32[]{:S(2)}) async-start(), calls=%async_computation.1 | async-start | bytes 131072 | tf_op jit(solution)/shard_map/while/body/eval_jaxpr/psum | solution.py:48
  339.0 1.2 copy-start
  426.3 17.9 %collective-permute-start = (f32[4096,64]{0,1:T(8,128)S(1)}, f32[4096,64]{0,1:T(8,128)S(1)}, u32[]{:S(2)}, u32[]{:S(2)}) collective-permute-start(f32[4096,64]{0,1:T(8,128)S(1)} %get-tuple-element.59), channel_id=1, source_target_pairs={{15,0},{0,1},{1,2},{2,3},{3,4},{4,5},{5,6},{6,7},{7,8},{8,9},{9,10... | collective-permute-start | bytes 3145736 | tf_op jit(solution)/shard_map/while/body/eval_jaxpr/ppermute | solution.py:12
  444.3 1.0 copy-start.1
  445.2 74.0 %all-reduce.5.cloned.1.call-start = ((), (), s32[]{:S(2)}) async-start(), calls=%async_computation.1 | async-start | bytes 131072 | tf_op jit(solution)/shard_map/while/body/eval_jaxpr/psum | solution.py:48
  445.2 1.2 copy-start
  532.5 17.9 %collective-permute-start = (f32[4096,64]{0,1:T(8,128)S(1)}, f32[4096,64]{0,1:T(8,128)S(1)}, u32[]{:S(2)}, u32[]{:S(2)}) collective-permute-start(f32[4096,64]{0,1:T(8,128)S(1)} %get-tuple-element.59), channel_id=1, source_target_pairs={{15,0},{0,1},{1,2},{2,3},{3,4},{4,5},{5,6},{6,7},{7,8},{8,9},{9,10... | collective-permute-start | bytes 3145736 | tf_op jit(solution)/shard_map/while/body/eval_jaxpr/ppermute | solution.py:12
  550.5 1.0 copy-start.1
  551.4 74.0 %all-reduce.5.cloned.1.call-start = ((), (), s32[]{:S(2)}) async-start(), calls=%async_computation.1 | async-start | bytes 131072 | tf_op jit(solution)/shard_map/while/body/eval_jaxpr/psum | solution.py:48
  551.4 1.2 copy-start
  638.8 17.9 %collective-permute-start = (f32[4096,64]{0,1:T(8,128)S(1)}, f32[4096,64]{0,1:T(8,128)S(1)}, u32[]{:S(2)}, u32[]{:S(2)}) collective-permute-start(f32[4096,64]{0,1:T(8,128)S(1)} %get-tuple-element.59), channel_id=1, source_target_pairs={{15,0},{0,1},{1,2},{2,3},{3,4},{4,5},{5,6},{6,7},{7,8},{8,9},{9,10... | collective-permute-start | bytes 3145736 | tf_op jit(solution)/shard_map/while/body/eval_jaxpr/ppermute | solution.py:12
  656.7 1.0 copy-start.1
  657.6 74.0 %all-reduce.5.cloned.1.call-start = ((), (), s32[]{:S(2)}) async-start(), calls=%async_computation.1 | async-start | bytes 131072 | tf_op jit(solution)/shard_map/while/body/eval_jaxpr/psum | solution.py:48
  657.6 1.2 copy-start
  744.9 17.9 %collective-permute-start = (f32[4096,64]{0,1:T(8,128)S(1)}, f32[4096,64]{0,1:T(8,128)S(1)}, u32[]{:S(2)}, u32[]{:S(2)}) collective-permute-start(f32[4096,64]{0,1:T(8,128)S(1)} %get-tuple-element.59), channel_id=1, source_target_pairs={{15,0},{0,1},{1,2},{2,3},{3,4},{4,5},{5,6},{6,7},{7,8},{8,9},{9,10... | collective-permute-start | bytes 3145736 | tf_op jit(solution)/shard_map/while/body/eval_jaxpr/ppermute | solution.py:12
  762.9 1.0 copy-start.1
  763.8 74.0 %all-reduce.5.cloned.1.call-start = ((), (), s32[]{:S(2)}) async-start(), calls=%async_computation.1 | async-start | bytes 131072 | tf_op jit(solution)/shard_map/while/body/eval_jaxpr/psum | solution.py:48
  763.8 1.2 copy-start
  851.2 17.9 %collective-permute-start = (f32[4096,64]{0,1:T(8,128)S(1)}, f32[4096,64]{0,1:T(8,128)S(1)}, u32[]{:S(2)}, u32[]{:S(2)}) collective-permute-start(f32[4096,64]{0,1:T(8,128)S(1)} %get-tuple-element.59), channel_id=1, source_target_pairs={{15,0},{0,1},{1,2},{2,3},{3,4},{4,5},{5,6},{6,7},{7,8},{8,9},{9,10... | collective-permute-start | bytes 3145736 | tf_op jit(solution)/shard_map/while/body/eval_jaxpr/ppermute | solution.py:12
  869.1 1.0 copy-start.1
  870.0 74.0 %all-reduce.5.cloned.1.call-start = ((), (), s32[]{:S(2)}) async-start(), calls=%async_computation.1 | async-start | bytes 131072 | tf_op jit(solution)/shard_map/while/body/eval_jaxpr/psum | solution.py:48
  870.0 1.2 copy-start
  957.4 17.9 %collective-permute-start = (f32[4096,64]{0,1:T(8,128)S(1)}, f32[4096,64]{0,1:T(8,128)S(1)}, u32[]{:S(2)}, u32[]{:S(2)}) collective-permute-start(f32[4096,64]{0,1:T(8,128)S(1)} %get-tuple-element.59), channel_id=1, source_target_pairs={{15,0},{0,1},{1,2},{2,3},{3,4},{4,5},{5,6},{6,7},{7,8},{8,9},{9,10... | collective-permute-start | bytes 3145736 | tf_op jit(solution)/shard_map/while/body/eval_jaxpr/ppermute | solution.py:12
  975.3 1.0 copy-start.1
  976.2 74.0 %all-reduce.5.cloned.1.call-start = ((), (), s32[]{:S(2)}) async-start(), calls=%async_computation.1 | async-start | bytes 131072 | tf_op jit(solution)/shard_map/while/body/eval_jaxpr/psum | solution.py:48
  976.2 1.2 copy-start
  1063.6 17.9 %collective-permute-start = (f32[4096,64]{0,1:T(8,128)S(1)}, f32[4096,64]{0,1:T(8,128)S(1)}, u32[]{:S(2)}, u32[]{:S(2)}) collective-permute-start(f32[4096,64]{0,1:T(8,128)S(1)} %get-tuple-element.59), channel_id=1, source_target_pairs={{15,0},{0,1},{1,2},{2,3},{3,4},{4,5},{5,6},{6,7},{7,8},{8,9},{9,10... | collective-permute-start | bytes 3145736 | tf_op jit(solution)/shard_map/while/body/eval_jaxpr/ppermute | solution.py:12
  1081.5 1.0 copy-start.1
  1082.4 74.0 %all-reduce.5.cloned.1.call-start = ((), (), s32[]{:S(2)}) async-start(), calls=%async_computation.1 | async-start | bytes 131072 | tf_op jit(solution)/shard_map/while/body/eval_jaxpr/psum | solution.py:48
  1082.4 1.2 copy-start
  1169.8 17.9 %collective-permute-start = (f32[4096,64]{0,1:T(8,128)S(1)}, f32[4096,64]{0,1:T(8,128)S(1)}, u32[]{:S(2)}, u32[]{:S(2)}) collective-permute-start(f32[4096,64]{0,1:T(8,128)S(1)} %get-tuple-element.59), channel_id=1, source_target_pairs={{15,0},{0,1},{1,2},{2,3},{3,4},{4,5},{5,6},{6,7},{7,8},{8,9},{9,10... | collective-permute-start | bytes 3145736 | tf_op jit(solution)/shard_map/while/body/eval_jaxpr/ppermute | solution.py:12
  1187.7 1.0 copy-start.1
  1188.6 74.0 %all-reduce.5.cloned.1.call-start = ((), (), s32[]{:S(2)}) async-start(), calls=%async_computation.1 | async-start | bytes 131072 | tf_op jit(solution)/shard_map/while/body/eval_jaxpr/psum | solution.py:48
  1188.6 1.2 copy-start
  1276.0 17.9 %collective-permute-start = (f32[4096,64]{0,1:T(8,128)S(1)}, f32[4096,64]{0,1:T(8,128)S(1)}, u32[]{:S(2)}, u32[]{:S(2)}) collective-permute-start(f32[4096,64]{0,1:T(8,128)S(1)} %get-tuple-element.59), channel_id=1, source_target_pairs={{15,0},{0,1},{1,2},{2,3},{3,4},{4,5},{5,6},{6,7},{7,8},{8,9},{9,10... | collective-permute-start | bytes 3145736 | tf_op jit(solution)/shard_map/while/body/eval_jaxpr/ppermute | solution.py:12
  1293.9 1.0 copy-start.1
  1294.8 74.0 %all-reduce.5.cloned.1.call-start = ((), (), s32[]{:S(2)}) async-start(), calls=%async_computation.1 | async-start | bytes 131072 | tf_op jit(solution)/shard_map/while/body/eval_jaxpr/psum | solution.py:48
  1294.8 1.2 copy-start
  1382.2 17.9 %collective-permute-start = (f32[4096,64]{0,1:T(8,128)S(1)}, f32[4096,64]{0,1:T(8,128)S(1)}, u32[]{:S(2)}, u32[]{:S(2)}) collective-permute-start(f32[4096,64]{0,1:T(8,128)S(1)} %get-tuple-element.59), channel_id=1, source_target_pairs={{15,0},{0,1},{1,2},{2,3},{3,4},{4,5},{5,6},{6,7},{7,8},{8,9},{9,10... | collective-permute-start | bytes 3145736 | tf_op jit(solution)/shard_map/while/body/eval_jaxpr/ppermute | solution.py:12
  1400.1 1.0 copy-start.1
  1401.0 74.0 %all-reduce.5.cloned.1.call-start = ((), (), s32[]{:S(2)}) async-start(), calls=%async_computation.1 | async-start | bytes 131072 | tf_op jit(solution)/shard_map/while/body/eval_jaxpr/psum | solution.py:48
  1401.0 1.2 copy-start
  1488.4 17.9 %collective-permute-start = (f32[4096,64]{0,1:T(8,128)S(1)}, f32[4096,64]{0,1:T(8,128)S(1)}, u32[]{:S(2)}, u32[]{:S(2)}) collective-permute-start(f32[4096,64]{0,1:T(8,128)S(1)} %get-tuple-element.59), channel_id=1, source_target_pairs={{15,0},{0,1},{1,2},{2,3},{3,4},{4,5},{5,6},{6,7},{7,8},{8,9},{9,10... | collective-permute-start | bytes 3145736 | tf_op jit(solution)/shard_map/while/body/eval_jaxpr/ppermute | solution.py:12
  1506.3 1.0 copy-start.1
  1507.2 1.2 copy-start.2
  1507.2 75.3 %all-reduce.3.cloned.1.call-start = ((), (), s32[]{:S(2)}) async-start(), calls=%async_computation | async-start | bytes 131072 | tf_op jit(solution)/shard_map/psum | solution.py:48
  1508.5 1.3 copy-start.3
  1589.3 4.5 copy-start.4
  1595.9 23.7 %collective-permute-start.1 = (f32[4096,64]{0,1:T(8,128)S(1)}, f32[4096,64]{0,1:T(8,128)S(1)}, u32[]{:S(2)}, u32[]{:S(2)}) collective-permute-start(f32[4096,64]{0,1:T(8,128)S(1)} %get-tuple-element.34), channel_id=1, source_target_pairs={{14,0},{15,1},{0,2},{1,3},{2,4},{3,5},{4,6},{5,7},{6,8},{7,9},{8,1... | collective-permute-start | bytes 3145736 | tf_op jit(solution)/shard_map/ppermute | solution.py:12
Sparse Core Ops, SparseCore 0:
  19.2 75.2 all-reduce.4
  130.5 70.1 all-reduce.4
  236.7 70.1 all-reduce.4
  342.9 70.1 all-reduce.4
  449.1 70.1 all-reduce.4
  555.3 70.1 all-reduce.4
  661.5 70.1 all-reduce.4
  767.7 70.1 all-reduce.4
  873.9 70.1 all-reduce.4
  980.1 70.1 all-reduce.4
  1086.3 70.1 all-reduce.4
  1192.5 70.1 all-reduce.4
  1298.7 70.1 all-reduce.4
  1404.9 70.1 all-reduce.4
Sparse Core Ops, SparseCore 1:
  1512.4 70.1 all-reduce.2
where the time goes:
time: 1630 us
  waiting for transfers between devices  1330 us (82%)
  matrix products  200 us (12%)
  local copies, waits for them, and re-layouts  75.6 us (5%)
    psum x15, waiting for transfers between devices, full_gram(): return (pair, lax.psum(inner_rows(pair, pair), 'rows'))  1060 us
    ppermute x15, waiting for transfers between devices, shifted(): return lax.ppermute(block, axis, route)  270 us
    dot_general x180, matrix products, lowdin(): jnp.dot(zmat, ymat, precision=lax.Precision.HIGHEST)  50.3 us
    dot_general x165, matrix products, lowdin(): ymat = jnp.dot(ymat, middle, precision=lax.Precision.HIGHEST)  46.9 us
    dot_general x15, matrix products, inner_rows(): lax.dot_general(left, right, (((0,), (0,)), ((), ())), precision=lax.Prec...  36.4 us
    dot_general x180, matrix products, lowdin(): zmat = jnp.dot(middle, zmat, precision=lax.Precision.HIGHEST)  36.2 us
  transfers between devices with their start and end apart: 30, of which 30 were waited for; matrix products, arithmetic and copies ran while one was open for 0% of the time, Pallas kernels for 0%

commit v1 on v0

v1 whole, which is shorter than its diff:
```python
import functools

import jax
import jax.numpy as jnp
from jax import lax
from jax.experimental import pallas as pl
from jax.experimental.pallas import tpu as pltpu
from jax.sharding import PartitionSpec as P

NS_STEPS = 12
F32 = jnp.float32
BF16 = jnp.bfloat16


def halves(x):
    hi = x.astype(BF16)
    lo = (x - hi.astype(F32)).astype(BF16)
    return hi, lo


def thirds(x):
    hi = x.astype(BF16)
    rest = x - hi.astype(F32)
    mid = rest.astype(BF16)
    lo = (rest - mid.astype(F32)).astype(BF16)
    return hi, mid, lo


def beside(*parts):
    return jnp.concatenate(parts, axis=1)


def above(*parts):
    return jnp.concatenate(parts, axis=0)


def mm(a, b):
    return jnp.dot(a, b, preferred_element_type=F32)


def tdot(a, b):
    return lax.dot_general(a, b, (((0,), (0,)), ((), ())), preferred_element_type=F32)


def product(a, b):
    ah, am, al = a
    bh, bm, bl = b
    n = bh.shape[1]
    top = beside(bh, bm)
    one = mm(beside(ah, am), above(top, top))
    two = mm(beside(ah, al), above(bl, bh))
    return one[:, :n] + (one[:, n:] + two)


def eye_of(n):
    i = lax.broadcasted_iota(jnp.int32, (n, n), 0)
    j = lax.broadcasted_iota(jnp.int32, (n, n), 1)
    return (i == j).astype(F32)


def lowdin(gram):
    n = gram.shape[0]
    eye = eye_of(n)
    diag = gram * eye
    down = 1.0 / jnp.sqrt(jnp.sum(diag, axis=1, keepdims=True))
    across = 1.0 / jnp.sqrt(jnp.sum(diag, axis=0, keepdims=True))
    y = gram * down * across
    z = eye
    for step in range(NS_STEPS):
        ys, zs = thirds(y), thirds(z)
        m = 1.5 * eye - 0.5 * product(zs, ys)
        ms = thirds(m)
        y = product(ys, ms)
        z = product(ms, zs)
    return down * z / across


def gram_kernel(top_ref, bottom_ref, out_ref):
    w = top_ref.shape[1] // 2
    th, tl = halves(top_ref[...])
    bh, bl = halves(bottom_ref[...])
    hi, lo = beside(th, bh), beside(tl, bl)
    full = (tdot(hi, hi) + tdot(lo, lo)) + (tdot(hi, lo) + tdot(lo, hi))

    def fold(i, j):
        i, j = i * 2 * w, j * 2 * w
        return full[i : i + w, j : j + w] + full[i + w : i + 2 * w, j + w : j + 2 * w]

    out_ref[...] = above(beside(fold(0, 0), fold(0, 1)), beside(fold(1, 0), fold(1, 1)))


def rotate_kernel(gram_ref, top_ref, bottom_ref, new_top_ref, new_bottom_ref):
    w = top_ref.shape[1] // 2
    weights = lowdin(gram_ref[...])
    zero = jnp.zeros((w, w), F32)

    def twice(block):
        return above(beside(block, zero), beside(zero, block))

    wide = above(
        beside(twice(weights[:w, :w]), twice(weights[:w, w:])),
        beside(twice(weights[w:, :w]), twice(weights[w:, w:])),
    )
    wh, wl = halves(wide)
    rows = top_ref.shape[0]
    chunk = 512
    for i in range(rows // chunk):
        at = pl.ds(i * chunk, chunk)
        ph, plo = halves(beside(top_ref[at, :], bottom_ref[at, :]))
        fresh = mm(ph, wh) + (mm(ph, wl) + mm(plo, wh))
        new_top_ref[at, :] = fresh[:, : 2 * w]
        new_bottom_ref[at, :] = fresh[:, 2 * w :]


VMEM = pl.BlockSpec(memory_space=pltpu.VMEM)
PARAMS = pltpu.CompilerParams(vmem_limit_bytes=32 * 1024 * 1024)


def gram_of(top, bottom):
    n = top.shape[1]
    return pl.pallas_call(
        gram_kernel,
        out_shape=jax.ShapeDtypeStruct((n, n), F32),
        in_specs=[VMEM] * 2,
        out_specs=VMEM,
        compiler_params=PARAMS,
    )(top, bottom)


def rotate(gram, top, bottom):
    return pl.pallas_call(
        rotate_kernel,
        out_shape=[jax.ShapeDtypeStruct(top.shape, F32)] * 2,
        in_specs=[VMEM] * 3,
        out_specs=[VMEM] * 2,
        compiler_params=PARAMS,
    )(gram, top, bottom)


def shifted(block, axis, distance):
    n = lax.axis_size(axis)
    return lax.ppermute(block, axis, [((i - distance) % n, i) for i in range(n)])


def row_sum(part):
    n = lax.axis_size("rows")
    inner = 4
    total = part
    for d in range(1, inner):
        route = [(i, i - i % inner + (i + d) % inner) for i in range(n)]
        total = total + lax.ppermute(part, "rows", route)
    return total + lax.ppermute(total, "rows", [(i, (i + inner) % n) for i in range(n)])


def packed(block):
    half = block.shape[0] // 2
    return jnp.concatenate([block[:half], block[half:]], axis=1)


def unpacked(block):
    half = block.shape[1] // 2
    return jnp.concatenate([block[:, :half], block[:, half:]], axis=0)


def on_device(snapshots):
    width = snapshots.shape[1] // 2
    top = packed(snapshots[:, :width])
    bottom = packed(snapshots[:, width:])
    rounds = lax.axis_size("cols") - 1
    for r in range(rounds):
        gram = row_sum(gram_of(top, bottom))
        top, bottom = rotate(gram, top, bottom)
        bottom = shifted(bottom, "cols", 1 if r + 1 < rounds else 2)
    return jnp.concatenate([unpacked(top), unpacked(bottom)], axis=1)


def solution(mesh):
    return jax.shard_map(
        on_device, mesh=mesh, in_specs=(P("rows", "cols"),), out_specs=P("rows", "cols"), check_vma=False
    )
```

time: 1630 us -> 584 us (0.36)
  waiting for transfers between devices: 1330 us -> 391 us
  matrix products: 200 us -> 0 us
  Pallas kernels: 0 us -> 103 us
  local copies, waits for them, and re-layouts: 75.6 us -> 3.57 us
  starting transfers between devices: 3.83 us -> 75.6 us
    psum x15 -> x0, waiting for transfers between devices: 1060 us -> none  [full_gram(): return (pair, lax.psum(inner_rows(pair, pair), 'rows'))]
    dot_general x555 -> x0, matrix products: 200 us -> none  [the longest x180 50.3 us: lowdin(): jnp.dot(zmat, ymat, precision=lax.Precision.HIGHEST)]
    ppermute x15 -> x75, waiting for transfers between devices: 270 us -> 391 us  [the longest x15 274 us: shifted(): lax.ppermute(block, axis, [((i - distance) % n, i) for i in range(n)])]
    pallas_call x0 -> x30, Pallas kernels: none -> 103 us  [the longest x15 81.8 us: rotate(): pl.pallas_call(rotate_kernel, out_shape=[jax.ShapeDtypeStruct(top.shape,...]
    ppermute x15 -> x75, starting transfers between devices: 3.8 us -> 75.6 us  [the longest x45 45.6 us: row_sum(): total = total + lax.ppermute(part, 'rows', route)]
    while x70 -> x0, local copies, waits for them, and re-layouts: 30.6 us -> none
    gather x15 -> x0, local copies, waits for them, and re-layouts: 29.1 us -> none  [lowdin(): diag = jnp.diagonal(gram)]
  transfers between devices with their start and end apart: 30 -> 75, of which waited for: 30 -> 75; matrix products, arithmetic and copies ran while one was open for 0% -> 0% of each run, Pallas kernels for 0% -> 0%
where the time goes in v1:
time: 584 us; the launch traced here: 577 us
  waiting for transfers between devices  391 us (67%)
  Pallas kernels  103 us (18%)
  starting transfers between devices  75.6 us (13%)
    ppermute x15, waiting for transfers between devices, shifted(): lax.ppermute(block, axis, [((i - distance) % n, i) for i in range(n)])  274 us
    pallas_call x15, Pallas kernels, rotate(): pl.pallas_call(rotate_kernel, out_shape=[jax.ShapeDtypeStruct(top.shape,...  81.8 us
    ppermute x45, waiting for transfers between devices, row_sum(): total = total + lax.ppermute(part, 'rows', route)  73.4 us
    ppermute x45, starting transfers between devices, row_sum(): total = total + lax.ppermute(part, 'rows', route)  45.6 us
    ppermute x15, waiting for transfers between devices, row_sum(): lax.ppermute(total, 'rows', [(i, (i + inner) % n) for i in range(n)])  44 us
    ppermute x15, starting transfers between devices, row_sum(): lax.ppermute(total, 'rows', [(i, (i + inner) % n) for i in range(n)])  28.9 us
    pallas_call x15, Pallas kernels, gram_of(): pl.pallas_call(gram_kernel, out_shape=jax.ShapeDtypeStruct((n, n), F32),...  21.2 us
  transfers between devices with their start and end apart: 75, of which 75 were waited for; matrix products, arithmetic and copies ran while one was open for 0% of the time, Pallas kernels for 0%

profile of v1, /device:TPU:0, one launch (start us, length us, event | category | flops | bytes accessed | tf_op | source)
XLA Modules:
  0.0 577.0 jit_solution(8054605539773697742)
XLA Ops:
  0.0 2.9 fusion
  4.9 3.2 collective-permute-start.2
  10.3 3.7 collective-permute-done.1
  16.2 2.8 collective-permute-done.3
  19.0 5.5 shard_map.18
  24.5 17.8 %collective-permute-done.4.bottom_ref = f32[2048,128]{1,0:T(8,128)S(1)} collective-permute-done((f32[2048,128]{1,0:T(8,128)S(1)}, f32[2048,128]{1,0:T(8,128)S(1)}, u32[]{:S(2)}, u32[]{:S(2)}) %collective-permute-start.4) | collective-permute-done | bytes 1048608 | tf_op jit(solution)/shard_map/ppermute | solution.py:142
  52.9 2.8 collective-permute-done.8
  55.7 5.5 shard_map.20
  61.2 17.8 %collective-permute-done.9.bottom_ref = f32[2048,128]{1,0:T(8,128)S(1)} collective-permute-done((f32[2048,128]{1,0:T(8,128)S(1)}, f32[2048,128]{1,0:T(8,128)S(1)}, u32[]{:S(2)}, u32[]{:S(2)}) %collective-permute-start.9) | collective-permute-done | bytes 1048608 | tf_op jit(solution)/shard_map/ppermute | solution.py:142
  85.0 3.3 collective-permute-done.11
  90.5 2.8 collective-permute-done.13
  93.3 5.5 shard_map.22
  98.9 17.8 %collective-permute-done.14.bottom_ref = f32[2048,128]{1,0:T(8,128)S(1)} collective-permute-done((f32[2048,128]{1,0:T(8,128)S(1)}, f32[2048,128]{1,0:T(8,128)S(1)}, u32[]{:S(2)}, u32[]{:S(2)}) %collective-permute-start.14) | collective-permute-done | bytes 1048608 | tf_op jit(solution)/shard_map/ppermute | solution.py:142
  127.0 2.8 collective-permute-done.18
  129.8 5.5 shard_map.24
  135.3 17.8 %collective-permute-done.19.bottom_ref = f32[2048,128]{1,0:T(8,128)S(1)} collective-permute-done((f32[2048,128]{1,0:T(8,128)S(1)}, f32[2048,128]{1,0:T(8,128)S(1)}, u32[]{:S(2)}, u32[]{:S(2)}) %collective-permute-start.19) | collective-permute-done | bytes 1048608 | tf_op jit(solution)/shard_map/ppermute | solution.py:142
  159.1 3.3 collective-permute-done.21
  164.6 2.8 collective-permute-done.23
  167.4 5.5 shard_map.26
  172.9 17.8 %collective-permute-done.24.bottom_ref = f32[2048,128]{1,0:T(8,128)S(1)} collective-permute-done((f32[2048,128]{1,0:T(8,128)S(1)}, f32[2048,128]{1,0:T(8,128)S(1)}, u32[]{:S(2)}, u32[]{:S(2)}) %collective-permute-start.24) | collective-permute-done | bytes 1048608 | tf_op jit(solution)/shard_map/ppermute | solution.py:142
  196.5 2.1 collective-permute-done.26
  201.1 2.8 collective-permute-done.28
  203.9 5.5 shard_map.28
  209.4 17.8 %collective-permute-done.29.bottom_ref = f32[2048,128]{1,0:T(8,128)S(1)} collective-permute-done((f32[2048,128]{1,0:T(8,128)S(1)}, f32[2048,128]{1,0:T(8,128)S(1)}, u32[]{:S(2)}, u32[]{:S(2)}) %collective-permute-start.29) | collective-permute-done | bytes 1048608 | tf_op jit(solution)/shard_map/ppermute | solution.py:142
  233.2 3.3 collective-permute-done.31
  238.7 2.8 collective-permute-done.33
  241.5 5.5 shard_map.30
  247.0 17.8 %collective-permute-done.34.bottom_ref = f32[2048,128]{1,0:T(8,128)S(1)} collective-permute-done((f32[2048,128]{1,0:T(8,128)S(1)}, f32[2048,128]{1,0:T(8,128)S(1)}, u32[]{:S(2)}, u32[]{:S(2)}) %collective-permute-start.34) | collective-permute-done | bytes 1048608 | tf_op jit(solution)/shard_map/ppermute | solution.py:142
  273.4 2.4 collective-permute-start.38
  275.8 2.7 collective-permute-done.38
  278.5 5.4 shard_map.32
  284.0 17.8 %collective-permute-done.39.bottom_ref = f32[2048,128]{1,0:T(8,128)S(1)} collective-permute-done((f32[2048,128]{1,0:T(8,128)S(1)}, f32[2048,128]{1,0:T(8,128)S(1)}, u32[]{:S(2)}, u32[]{:S(2)}) %collective-permute-start.39) | collective-permute-done | bytes 1048608 | tf_op jit(solution)/shard_map/ppermute | solution.py:142
  303.2 2.3 collective-permute-start.42
  308.1 3.3 collective-permute-done.41
  314.0 3.1 collective-permute-done.43
  317.2 5.5 shard_map.34
  322.7 18.3 %collective-permute-done.44.bottom_ref = f32[2048,128]{1,0:T(8,128)S(1)} collective-permute-done((f32[2048,128]{1,0:T(8,128)S(1)}, f32[2048,128]{1,0:T(8,128)S(1)}, u32[]{:S(2)}, u32[]{:S(2)}) %collective-permute-start.44) | collective-permute-done | bytes 1048608 | tf_op jit(solution)/shard_map/ppermute | solution.py:142
  349.4 2.4 collective-permute-start.48
  351.8 3.0 collective-permute-done.48
  354.9 5.5 shard_map.36
  360.4 18.5 %collective-permute-done.49.bottom_ref = f32[2048,128]{1,0:T(8,128)S(1)} collective-permute-done((f32[2048,128]{1,0:T(8,128)S(1)}, f32[2048,128]{1,0:T(8,128)S(1)}, u32[]{:S(2)}, u32[]{:S(2)}) %collective-permute-start.49) | collective-permute-done | bytes 1048608 | tf_op jit(solution)/shard_map/ppermute | solution.py:142
  380.4 2.1 collective-permute-start.52
  385.0 3.3 collective-permute-done.51
  388.9 2.1 collective-permute-start.53
  391.0 3.0 collective-permute-done.53
  394.1 5.5 shard_map.38
  399.6 18.5 %collective-permute-done.54.bottom_ref = f32[2048,128]{1,0:T(8,128)S(1)} collective-permute-done((f32[2048,128]{1,0:T(8,128)S(1)}, f32[2048,128]{1,0:T(8,128)S(1)}, u32[]{:S(2)}, u32[]{:S(2)}) %collective-permute-start.54) | collective-permute-done | bytes 1048608 | tf_op jit(solution)/shard_map/ppermute | solution.py:142
  426.7 2.3 collective-permute-start.58
  429.0 3.0 collective-permute-done.58
  432.0 5.5 shard_map.40
  437.6 18.5 %collective-permute-done.59.bottom_ref = f32[2048,128]{1,0:T(8,128)S(1)} collective-permute-done((f32[2048,128]{1,0:T(8,128)S(1)}, f32[2048,128]{1,0:T(8,128)S(1)}, u32[]{:S(2)}, u32[]{:S(2)}) %collective-permute-start.59) | collective-permute-done | bytes 1048608 | tf_op jit(solution)/shard_map/ppermute | solution.py:142
  462.0 3.3 collective-permute-done.61
  468.0 3.1 collective-permute-done.63
  471.1 5.5 shard_map.42
  476.6 18.5 %collective-permute-done.64.bottom_ref = f32[2048,128]{1,0:T(8,128)S(1)} collective-permute-done((f32[2048,128]{1,0:T(8,128)S(1)}, f32[2048,128]{1,0:T(8,128)S(1)}, u32[]{:S(2)}, u32[]{:S(2)}) %collective-permute-start.64) | collective-permute-done | bytes 1048608 | tf_op jit(solution)/shard_map/ppermute | solution.py:142
  500.9 2.1 collective-permute-done.66
  503.7 2.2 collective-permute-start.68
  505.9 3.1 collective-permute-done.68
  509.1 5.5 shard_map.44
  514.6 18.5 %collective-permute-done.69.bottom_ref = f32[2048,128]{1,0:T(8,128)S(1)} collective-permute-done((f32[2048,128]{1,0:T(8,128)S(1)}, f32[2048,128]{1,0:T(8,128)S(1)}, u32[]{:S(2)}, u32[]{:S(2)}) %collective-permute-start.69) | collective-permute-done | bytes 1048608 | tf_op jit(solution)/shard_map/ppermute | solution.py:142
  539.1 3.3 collective-permute-done.71
  544.8 3.4 collective-permute-done.73
  548.2 5.5 shard_map.46
  554.1 20.2 %collective-permute-done.74 = f32[2048,128]{1,0:T(8,128)S(1)} collective-permute-done((f32[2048,128]{1,0:T(8,128)S(1)}, f32[2048,128]{1,0:T(8,128)S(1)}, u32[]{:S(2)}, u32[]{:S(2)}) %collective-permute-start.74) | collective-permute-done | bytes 1048608 | tf_op jit(solution)/shard_map/ppermute | solution.py:142
  (151 shorter events, 124.1 us)
Async XLA Ops:
  4.9 5.3 collective-permute-start.2
  8.1 5.8 %collective-permute-start.1 = (f32[128,128]{1,0:T(8,128)S(1)}, f32[128,128]{1,0:T(8,128)S(1)}, u32[]{:S(2)}, u32[]{:S(2)}) collective-permute-start(f32[128,128]{1,0:T(8,128)S(1)} %shard_map.17), channel_id=1, source_target_pairs={{0,32},{16,48},{32,0},{48,16},{64,96},{80,112},{96,64},{112,80},{1... | collective-permute-start | bytes 196616 | tf_op jit(solution)/shard_map/ppermute | solution.py:151
  8.7 5.8 %collective-permute-start = (f32[128,128]{1,0:T(8,128)S(1)}, f32[128,128]{1,0:T(8,128)S(1)}, u32[]{:S(2)}, u32[]{:S(2)}) collective-permute-start(f32[128,128]{1,0:T(8,128)S(1)} %shard_map.17), channel_id=1, source_target_pairs={{0,16},{16,32},{32,48},{48,0},{64,80},{80,96},{96,112},{112,64},{1... | collective-permute-start | bytes 196616 | tf_op jit(solution)/shard_map/ppermute | solution.py:151
  24.4 17.9 %collective-permute-start.4 = (f32[2048,128]{1,0:T(8,128)S(1)}, f32[2048,128]{1,0:T(8,128)S(1)}, u32[]{:S(2)}, u32[]{:S(2)}) collective-permute-start(f32[2048,128]{1,0:T(8,128)S(1)} %get-tuple-element.36), channel_id=1, source_target_pairs={{15,0},{0,1},{1,2},{2,3},{3,4},{4,5},{5,6},{6,7},{7,8},{8,9},{9,10... | collective-permute-start | bytes 3145736 | tf_op jit(solution)/shard_map/ppermute | solution.py:142
  44.4 5.8 %collective-permute-start.6 = (f32[128,128]{1,0:T(8,128)S(1)}, f32[128,128]{1,0:T(8,128)S(1)}, u32[]{:S(2)}, u32[]{:S(2)}) collective-permute-start(f32[128,128]{1,0:T(8,128)S(1)} %shard_map.19), channel_id=1, source_target_pairs={{0,32},{16,48},{32,0},{48,16},{64,96},{80,112},{96,64},{112,80},{1... | collective-permute-start | bytes 196616 | tf_op jit(solution)/shard_map/ppermute | solution.py:151
  45.3 5.6 collective-permute-start.5
  50.9 4.8 collective-permute-start.8
  61.1 17.9 %collective-permute-start.9 = (f32[2048,128]{1,0:T(8,128)S(1)}, f32[2048,128]{1,0:T(8,128)S(1)}, u32[]{:S(2)}, u32[]{:S(2)}) collective-permute-start(f32[2048,128]{1,0:T(8,128)S(1)} %get-tuple-element.38), channel_id=1, source_target_pairs={{15,0},{0,1},{1,2},{2,3},{3,4},{4,5},{5,6},{6,7},{7,8},{8,9},{9,10... | collective-permute-start | bytes 3145736 | tf_op jit(solution)/shard_map/ppermute | solution.py:142
  80.5 4.5 collective-permute-start.12
  82.5 5.8 %collective-permute-start.11 = (f32[128,128]{1,0:T(8,128)S(1)}, f32[128,128]{1,0:T(8,128)S(1)}, u32[]{:S(2)}, u32[]{:S(2)}) collective-permute-start(f32[128,128]{1,0:T(8,128)S(1)} %shard_map.21), channel_id=1, source_target_pairs={{0,32},{16,48},{32,0},{48,16},{64,96},{80,112},{96,64},{112,80},{1... | collective-permute-start | bytes 196616 | tf_op jit(solution)/shard_map/ppermute | solution.py:151
  83.4 5.6 collective-permute-start.10
  98.8 17.9 %collective-permute-start.14 = (f32[2048,128]{1,0:T(8,128)S(1)}, f32[2048,128]{1,0:T(8,128)S(1)}, u32[]{:S(2)}, u32[]{:S(2)}) collective-permute-start(f32[2048,128]{1,0:T(8,128)S(1)} %get-tuple-element.40), channel_id=1, source_target_pairs={{15,0},{0,1},{1,2},{2,3},{3,4},{4,5},{5,6},{6,7},{7,8},{8,9},{9,10... | collective-permute-start | bytes 3145736 | tf_op jit(solution)/shard_map/ppermute | solution.py:142
  118.7 5.8 %collective-permute-start.16 = (f32[128,128]{1,0:T(8,128)S(1)}, f32[128,128]{1,0:T(8,128)S(1)}, u32[]{:S(2)}, u32[]{:S(2)}) collective-permute-start(f32[128,128]{1,0:T(8,128)S(1)} %shard_map.23), channel_id=1, source_target_pairs={{0,32},{16,48},{32,0},{48,16},{64,96},{80,112},{96,64},{112,80},{1... | collective-permute-start | bytes 196616 | tf_op jit(solution)/shard_map/ppermute | solution.py:151
  119.6 5.6 collective-permute-start.15
  125.2 4.5 collective-permute-start.18
  135.2 17.9 %collective-permute-start.19 = (f32[2048,128]{1,0:T(8,128)S(1)}, f32[2048,128]{1,0:T(8,128)S(1)}, u32[]{:S(2)}, u32[]{:S(2)}) collective-permute-start(f32[2048,128]{1,0:T(8,128)S(1)} %get-tuple-element.42), channel_id=1, source_target_pairs={{15,0},{0,1},{1,2},{2,3},{3,4},{4,5},{5,6},{6,7},{7,8},{8,9},{9,10... | collective-permute-start | bytes 3145736 | tf_op jit(solution)/shard_map/ppermute | solution.py:142
  154.5 4.5 collective-permute-start.22
  156.5 5.8 %collective-permute-start.21 = (f32[128,128]{1,0:T(8,128)S(1)}, f32[128,128]{1,0:T(8,128)S(1)}, u32[]{:S(2)}, u32[]{:S(2)}) collective-permute-start(f32[128,128]{1,0:T(8,128)S(1)} %shard_map.25), channel_id=1, source_target_pairs={{0,32},{16,48},{32,0},{48,16},{64,96},{80,112},{96,64},{112,80},{1... | collective-permute-start | bytes 196616 | tf_op jit(solution)/shard_map/ppermute | solution.py:151
  157.4 5.6 collective-permute-start.20
  172.8 17.9 %collective-permute-start.24 = (f32[2048,128]{1,0:T(8,128)S(1)}, f32[2048,128]{1,0:T(8,128)S(1)}, u32[]{:S(2)}, u32[]{:S(2)}) collective-permute-start(f32[2048,128]{1,0:T(8,128)S(1)} %get-tuple-element.44), channel_id=1, source_target_pairs={{15,0},{0,1},{1,2},{2,3},{3,4},{4,5},{5,6},{6,7},{7,8},{8,9},{9,10... | collective-permute-start | bytes 3145736 | tf_op jit(solution)/shard_map/ppermute | solution.py:142
  192.8 5.8 %collective-permute-start.26 = (f32[128,128]{1,0:T(8,128)S(1)}, f32[128,128]{1,0:T(8,128)S(1)}, u32[]{:S(2)}, u32[]{:S(2)}) collective-permute-start(f32[128,128]{1,0:T(8,128)S(1)} %shard_map.27), channel_id=1, source_target_pairs={{0,32},{16,48},{32,0},{48,16},{64,96},{80,112},{96,64},{112,80},{1... | collective-permute-start | bytes 196616 | tf_op jit(solution)/shard_map/ppermute | solution.py:151
  193.7 5.6 collective-permute-start.25
  199.3 4.6 collective-permute-start.28
  209.3 17.9 %collective-permute-start.29 = (f32[2048,128]{1,0:T(8,128)S(1)}, f32[2048,128]{1,0:T(8,128)S(1)}, u32[]{:S(2)}, u32[]{:S(2)}) collective-permute-start(f32[2048,128]{1,0:T(8,128)S(1)} %get-tuple-element.46), channel_id=1, source_target_pairs={{15,0},{0,1},{1,2},{2,3},{3,4},{4,5},{5,6},{6,7},{7,8},{8,9},{9,10... | collective-permute-start | bytes 3145736 | tf_op jit(solution)/shard_map/ppermute | solution.py:142
  228.6 4.5 collective-permute-start.32
  230.6 5.8 %collective-permute-start.31 = (f32[128,128]{1,0:T(8,128)S(1)}, f32[128,128]{1,0:T(8,128)S(1)}, u32[]{:S(2)}, u32[]{:S(2)}) collective-permute-start(f32[128,128]{1,0:T(8,128)S(1)} %shard_map.29), channel_id=1, source_target_pairs={{0,32},{16,48},{32,0},{48,16},{64,96},{80,112},{96,64},{112,80},{1... | collective-permute-start | bytes 196616 | tf_op jit(solution)/shard_map/ppermute | solution.py:151
  231.5 5.6 collective-permute-start.30
  247.0 17.9 %collective-permute-start.34 = (f32[2048,128]{1,0:T(8,128)S(1)}, f32[2048,128]{1,0:T(8,128)S(1)}, u32[]{:S(2)}, u32[]{:S(2)}) collective-permute-start(f32[2048,128]{1,0:T(8,128)S(1)} %get-tuple-element.48), channel_id=1, source_target_pairs={{15,0},{0,1},{1,2},{2,3},{3,4},{4,5},{5,6},{6,7},{7,8},{8,9},{9,10... | collective-permute-start | bytes 3145736 | tf_op jit(solution)/shard_map/ppermute | solution.py:142
  266.9 5.8 %collective-permute-start.36 = (f32[128,128]{1,0:T(8,128)S(1)}, f32[128,128]{1,0:T(8,128)S(1)}, u32[]{:S(2)}, u32[]{:S(2)}) collective-permute-start(f32[128,128]{1,0:T(8,128)S(1)} %shard_map.31), channel_id=1, source_target_pairs={{0,32},{16,48},{32,0},{48,16},{64,96},{80,112},{96,64},{112,80},{1... | collective-permute-start | bytes 196616 | tf_op jit(solution)/shard_map/ppermute | solution.py:151
  267.8 5.6 collective-permute-start.35
  273.4 5.0 collective-permute-start.38
  283.9 17.9 %collective-permute-start.39 = (f32[2048,128]{1,0:T(8,128)S(1)}, f32[2048,128]{1,0:T(8,128)S(1)}, u32[]{:S(2)}, u32[]{:S(2)}) collective-permute-start(f32[2048,128]{1,0:T(8,128)S(1)} %get-tuple-element.50), channel_id=1, source_target_pairs={{15,0},{0,1},{1,2},{2,3},{3,4},{4,5},{5,6},{6,7},{7,8},{8,9},{9,10... | collective-permute-start | bytes 3145736 | tf_op jit(solution)/shard_map/ppermute | solution.py:142
  303.2 4.9 collective-permute-start.42
  305.6 5.8 %collective-permute-start.41 = (f32[128,128]{1,0:T(8,128)S(1)}, f32[128,128]{1,0:T(8,128)S(1)}, u32[]{:S(2)}, u32[]{:S(2)}) collective-permute-start(f32[128,128]{1,0:T(8,128)S(1)} %shard_map.33), channel_id=1, source_target_pairs={{0,32},{16,48},{32,0},{48,16},{64,96},{80,112},{96,64},{112,80},{1... | collective-permute-start | bytes 196616 | tf_op jit(solution)/shard_map/ppermute | solution.py:151
  306.5 5.5 collective-permute-start.40
  312.1 5.1 collective-permute-start.43
  322.6 18.4 %collective-permute-start.44 = (f32[2048,128]{1,0:T(8,128)S(1)}, f32[2048,128]{1,0:T(8,128)S(1)}, u32[]{:S(2)}, u32[]{:S(2)}) collective-permute-start(f32[2048,128]{1,0:T(8,128)S(1)} %get-tuple-element.52), channel_id=1, source_target_pairs={{15,0},{0,1},{1,2},{2,3},{3,4},{4,5},{5,6},{6,7},{7,8},{8,9},{9,10... | collective-permute-start | bytes 3145736 | tf_op jit(solution)/shard_map/ppermute | solution.py:142
  342.6 5.8 %collective-permute-start.46 = (f32[128,128]{1,0:T(8,128)S(1)}, f32[128,128]{1,0:T(8,128)S(1)}, u32[]{:S(2)}, u32[]{:S(2)}) collective-permute-start(f32[128,128]{1,0:T(8,128)S(1)} %shard_map.35), channel_id=1, source_target_pairs={{0,32},{16,48},{32,0},{48,16},{64,96},{80,112},{96,64},{112,80},{1... | collective-permute-start | bytes 196616 | tf_op jit(solution)/shard_map/ppermute | solution.py:151
  343.9 5.5 collective-permute-start.45
  349.4 5.4 collective-permute-start.48
  360.3 18.6 %collective-permute-start.49 = (f32[2048,128]{1,0:T(8,128)S(1)}, f32[2048,128]{1,0:T(8,128)S(1)}, u32[]{:S(2)}, u32[]{:S(2)}) collective-permute-start(f32[2048,128]{1,0:T(8,128)S(1)} %get-tuple-element.54), channel_id=1, source_target_pairs={{15,0},{0,1},{1,2},{2,3},{3,4},{4,5},{5,6},{6,7},{7,8},{8,9},{9,10... | collective-permute-start | bytes 3145736 | tf_op jit(solution)/shard_map/ppermute | solution.py:142
  380.4 4.6 collective-permute-start.52
  382.4 5.8 %collective-permute-start.51 = (f32[128,128]{1,0:T(8,128)S(1)}, f32[128,128]{1,0:T(8,128)S(1)}, u32[]{:S(2)}, u32[]{:S(2)}) collective-permute-start(f32[128,128]{1,0:T(8,128)S(1)} %shard_map.37), channel_id=1, source_target_pairs={{0,32},{16,48},{32,0},{48,16},{64,96},{80,112},{96,64},{112,80},{1... | collective-permute-start | bytes 196616 | tf_op jit(solution)/shard_map/ppermute | solution.py:151
  383.4 5.6 collective-permute-start.50
  388.9 5.1 collective-permute-start.53
  399.5 18.6 %collective-permute-start.54 = (f32[2048,128]{1,0:T(8,128)S(1)}, f32[2048,128]{1,0:T(8,128)S(1)}, u32[]{:S(2)}, u32[]{:S(2)}) collective-permute-start(f32[2048,128]{1,0:T(8,128)S(1)} %get-tuple-element.56), channel_id=1, source_target_pairs={{15,0},{0,1},{1,2},{2,3},{3,4},{4,5},{5,6},{6,7},{7,8},{8,9},{9,10... | collective-permute-start | bytes 3145736 | tf_op jit(solution)/shard_map/ppermute | solution.py:142
  420.2 5.8 %collective-permute-start.56 = (f32[128,128]{1,0:T(8,128)S(1)}, f32[128,128]{1,0:T(8,128)S(1)}, u32[]{:S(2)}, u32[]{:S(2)}) collective-permute-start(f32[128,128]{1,0:T(8,128)S(1)} %shard_map.39), channel_id=1, source_target_pairs={{0,32},{16,48},{32,0},{48,16},{64,96},{80,112},{96,64},{112,80},{1... | collective-permute-start | bytes 196616 | tf_op jit(solution)/shard_map/ppermute | solution.py:151
  421.1 5.6 collective-permute-start.55
  426.7 5.3 collective-permute-start.58
  437.5 18.6 %collective-permute-start.59 = (f32[2048,128]{1,0:T(8,128)S(1)}, f32[2048,128]{1,0:T(8,128)S(1)}, u32[]{:S(2)}, u32[]{:S(2)}) collective-permute-start(f32[2048,128]{1,0:T(8,128)S(1)} %get-tuple-element.58), channel_id=1, source_target_pairs={{15,0},{0,1},{1,2},{2,3},{3,4},{4,5},{5,6},{6,7},{7,8},{8,9},{9,10... | collective-permute-start | bytes 3145736 | tf_op jit(solution)/shard_map/ppermute | solution.py:142
  457.5 4.5 collective-permute-start.62
  459.5 5.8 %collective-permute-start.61 = (f32[128,128]{1,0:T(8,128)S(1)}, f32[128,128]{1,0:T(8,128)S(1)}, u32[]{:S(2)}, u32[]{:S(2)}) collective-permute-start(f32[128,128]{1,0:T(8,128)S(1)} %shard_map.41), channel_id=1, source_target_pairs={{0,32},{16,48},{32,0},{48,16},{64,96},{80,112},{96,64},{112,80},{1... | collective-permute-start | bytes 196616 | tf_op jit(solution)/shard_map/ppermute | solution.py:151
  460.4 5.6 collective-permute-start.60
  466.0 5.1 collective-permute-start.63
  476.6 18.6 %collective-permute-start.64 = (f32[2048,128]{1,0:T(8,128)S(1)}, f32[2048,128]{1,0:T(8,128)S(1)}, u32[]{:S(2)}, u32[]{:S(2)}) collective-permute-start(f32[2048,128]{1,0:T(8,128)S(1)} %get-tuple-element.60), channel_id=1, source_target_pairs={{15,0},{0,1},{1,2},{2,3},{3,4},{4,5},{5,6},{6,7},{7,8},{8,9},{9,10... | collective-permute-start | bytes 3145736 | tf_op jit(solution)/shard_map/ppermute | solution.py:142
  497.2 5.8 %collective-permute-start.66 = (f32[128,128]{1,0:T(8,128)S(1)}, f32[128,128]{1,0:T(8,128)S(1)}, u32[]{:S(2)}, u32[]{:S(2)}) collective-permute-start(f32[128,128]{1,0:T(8,128)S(1)} %shard_map.43), channel_id=1, source_target_pairs={{0,32},{16,48},{32,0},{48,16},{64,96},{80,112},{96,64},{112,80},{1... | collective-permute-start | bytes 196616 | tf_op jit(solution)/shard_map/ppermute | solution.py:151
  498.1 5.6 collective-permute-start.65
  503.7 5.4 collective-permute-start.68
  514.6 18.6 %collective-permute-start.69 = (f32[2048,128]{1,0:T(8,128)S(1)}, f32[2048,128]{1,0:T(8,128)S(1)}, u32[]{:S(2)}, u32[]{:S(2)}) collective-permute-start(f32[2048,128]{1,0:T(8,128)S(1)} %get-tuple-element.62), channel_id=1, source_target_pairs={{15,0},{0,1},{1,2},{2,3},{3,4},{4,5},{5,6},{6,7},{7,8},{8,9},{9,10... | collective-permute-start | bytes 3145736 | tf_op jit(solution)/shard_map/ppermute | solution.py:142
  534.6 4.5 collective-permute-start.72
  536.6 5.8 %collective-permute-start.71 = (f32[128,128]{1,0:T(8,128)S(1)}, f32[128,128]{1,0:T(8,128)S(1)}, u32[]{:S(2)}, u32[]{:S(2)}) collective-permute-start(f32[128,128]{1,0:T(8,128)S(1)} %shard_map.45), channel_id=1, source_target_pairs={{0,32},{16,48},{32,0},{48,16},{64,96},{80,112},{96,64},{112,80},{1... | collective-permute-start | bytes 196616 | tf_op jit(solution)/shard_map/ppermute | solution.py:151
  537.5 5.6 collective-permute-start.70
  543.1 5.1 collective-permute-start.73
  553.6 20.6 %collective-permute-start.74 = (f32[2048,128]{1,0:T(8,128)S(1)}, f32[2048,128]{1,0:T(8,128)S(1)}, u32[]{:S(2)}, u32[]{:S(2)}) collective-permute-start(f32[2048,128]{1,0:T(8,128)S(1)} %get-tuple-element.64), channel_id=1, source_target_pairs={{14,0},{15,1},{0,2},{1,3},{2,4},{3,5},{4,6},{5,7},{6,8},{7,9},{8,1... | collective-permute-start | bytes 3145736 | tf_op jit(solution)/shard_map/ppermute | solution.py:142
  (11 other events, 47.7 us)

commit v2 on v0

v2 whole, which is shorter than its diff:
```python
import jax
import jax.numpy as jnp
from jax import lax
from jax.experimental import pallas as pl
from jax.experimental.pallas import tpu as pltpu
from jax.sharding import PartitionSpec as P

NS_STEPS = 12
BLK = 64
CHUNK = 512
F32 = jnp.float32
BF16 = jnp.bfloat16

FIRST = (((0, 2), (1, 3)), ((1, 2),))
MIDDLE = (((0, 3),), ((0, 2), (1, 3)), ((1, 2),))
LAST = (((0, 3),), ((0, 2), (1, 3)))


def halves(x):
    hi = x.astype(BF16)
    lo = (x - hi.astype(F32)).astype(BF16)
    return hi, lo


def beside(*parts):
    return jnp.concatenate(parts, axis=1)


def above(*parts):
    return jnp.concatenate(parts, axis=0)


def mm(a, b):
    return jnp.dot(a, b, preferred_element_type=F32)


def tdot(a, b):
    return lax.dot_general(a, b, (((0,), (0,)), ((), ())), preferred_element_type=F32)


def product(a, b):
    ah, al = a
    bh, bl = b
    n = bh.shape[1]
    row = beside(bh, bl)
    wide = mm(beside(ah, al), above(row, row))
    return wide[:, :n] + wide[:, n:]


def eye_of(n):
    i = lax.broadcasted_iota(jnp.int32, (n, n), 0)
    j = lax.broadcasted_iota(jnp.int32, (n, n), 1)
    return (i == j).astype(F32)


def lowdin(grams):
    eye = eye_of(2 * BLK)
    many = range(len(grams))
    down = [jnp.sqrt(jnp.sum(g * eye, axis=1, keepdims=True)) for g in grams]
    across = [jnp.sqrt(jnp.sum(g * eye, axis=0, keepdims=True)) for g in grams]
    e = [eye - grams[k] * (1.0 / down[k]) * (1.0 / across[k]) for k in many]
    z = [eye for k in many]
    for step in range(NS_STEPS):
        es = [halves(e[k]) for k in many]
        square = [product(es[k], es[k]) for k in many]
        z = [z[k] + 0.5 * (product(halves(z[k]), es[k]) if step else e[k]) for k in many]
        e = [0.75 * square[k] + 0.25 * product(halves(square[k]), es[k]) for k in many]
    weights = [z[k] * (1.0 / down[k]) * across[k] for k in many]
    turned = [z[k] * down[k] * (1.0 / across[k]) for k in many]
    fresh = [(eye - e[k]) * down[k] * across[k] for k in many]
    return weights, turned, fresh


def corners(block):
    w = BLK
    return ((block[:w, :w], block[:w, w:]), (block[w:, :w], block[w:, w:]))


class Gram:
    def __init__(self, tops, middle, bottoms):
        self.blocks = {}
        self.put((0, 1), (0, 1), tops)
        self.put((0, 1), (2, 3), middle)
        self.put((2, 3), (2, 3), bottoms)

    def put(self, rows, columns, block):
        cells = corners(block)
        for i, row in enumerate(rows):
            for j, column in enumerate(columns):
                if row <= column:
                    self.blocks[row, column] = cells[i][j]
                elif rows != columns:
                    self.blocks[column, row] = cells[i][j].T

    def cell(self, i, j):
        return self.blocks[i, j] if i <= j else self.blocks[j, i].T

    def get(self, rows, columns):
        return above(*[beside(*[self.cell(i, j) for j in columns]) for i in rows])


def wave(gram, levels, update_last):
    w = BLK
    zero = jnp.zeros((w, w), F32)
    unit = eye_of(w)
    columns = [above(*[unit if i == j else zero for i in range(4)]) for j in range(4)]
    for n, level in enumerate(levels):
        weights, turned, fresh = lowdin([gram.get(p, p) for p in level])
        for k, (t, b) in enumerate(level):
            if n == 0:
                (tt, tb), (bt, bb) = corners(weights[k])
                columns[t] = above(*[{t: tt, b: bt}.get(i, zero) for i in range(4)])
                columns[b] = above(*[{t: tb, b: bb}.get(i, zero) for i in range(4)])
            else:
                both = product(halves(beside(columns[t], columns[b])), halves(weights[k]))
                columns[t], columns[b] = both[:, :w], both[:, w:]
        if n + 1 == len(levels) and not update_last:
            break
        p = level[0]
        q = level[1] if len(level) > 1 else (1 - p[0], 5 - p[1])
        mixed = product(halves(turned[0]), halves(gram.get(p, q)))
        if len(level) > 1:
            mixed = product(halves(mixed), halves(weights[1]))
        gram.put(p, q, mixed)
        for k, pair in enumerate(level):
            gram.put(pair, pair, fresh[k])
    return beside(*columns)


def finish(gram, levels, urgent_ref, message_ref, tops_ref):
    w = 2 * BLK
    weights = wave(gram, levels, tops_ref is not None)
    message_ref[...] = weights[:, :w]
    urgent_ref[: 2 * w, :] = weights[:, w:]
    if tops_ref is not None:
        urgent_ref[2 * w :, :] = gram.get((2, 3), (2, 3))
        tops_ref[...] = gram.get((0, 1), (0, 1))


def first_wave_kernel(near_ref, far_ref, *outs):
    w = 2 * BLK
    sums = near_ref[...] + far_ref[...]
    finish(Gram(sums[:w, :], sums[w : 2 * w, :], sums[2 * w :, :]), FIRST, *outs)


def held_gram(near_ref, far_ref, old_tops_ref, old_urgent_ref):
    return Gram(old_tops_ref[...], near_ref[...] + far_ref[...], old_urgent_ref[4 * BLK :, :])


def wave_kernel(near_ref, far_ref, old_tops_ref, old_urgent_ref, *outs):
    finish(held_gram(near_ref, far_ref, old_tops_ref, old_urgent_ref), MIDDLE, *outs)


def last_wave_kernel(near_ref, far_ref, old_tops_ref, old_urgent_ref, urgent_ref, message_ref):
    finish(held_gram(near_ref, far_ref, old_tops_ref, old_urgent_ref), LAST, urgent_ref, message_ref, None)


def rotated(pair, wide):
    ph, plo = halves(pair)
    wh, wl = wide
    return mm(ph, wh) + (mm(ph, wl) + mm(plo, wh))


def cross(left, right):
    lh, ll = halves(left)
    rh, rl = halves(right)
    n = left.shape[1]
    wide = tdot(beside(lh, ll), beside(rh, rl))
    return (wide[:n, :n] + wide[n:, n:]) + (wide[:n, n:] + wide[n:, :n])


def chunks(ref):
    return [pl.ds(i * CHUNK, CHUNK) for i in range(ref.shape[0] // CHUNK)]


def first_gram_kernel(top_ref, bottom_ref, out_ref):
    w = 2 * BLK
    parts = None
    for at in chunks(top_ref):
        top, bottom = top_ref[at, :], bottom_ref[at, :]
        more = (cross(top, top), cross(top, bottom), cross(bottom, bottom))
        parts = more if parts is None else [a + b for a, b in zip(parts, more)]
    for i in range(3):
        out_ref[i * w : (i + 1) * w, :] = parts[i]


def side_kernel(weights_ref, top_ref, bottom_ref, out_ref):
    n = weights_ref.shape[0]
    wide = halves(weights_ref[n - 4 * BLK :, :])
    for at in chunks(top_ref):
        out_ref[at, :] = rotated(beside(top_ref[at, :], bottom_ref[at, :]), wide)


def bottom_kernel(weights_ref, message_ref, left_ref, bottom_ref, top_ref, new_bottom_ref, part_ref):
    wide = halves(weights_ref[: 4 * BLK, :])
    new_bottom_ref[top_ref.shape[0] :, :] = message_ref[...]
    part = None
    for at in chunks(top_ref):
        fresh = rotated(beside(left_ref[at, :], bottom_ref[at, :]), wide)
        new_bottom_ref[at, :] = fresh
        more = cross(top_ref[at, :], fresh)
        part = more if part is None else part + more
    part_ref[...] = part


VMEM = pl.BlockSpec(memory_space=pltpu.VMEM)
PARAMS = pltpu.CompilerParams(vmem_limit_bytes=32 * 1024 * 1024)


def call(kernel, shapes, *operands):
    out = pl.pallas_call(
        kernel,
        out_shape=[jax.ShapeDtypeStruct(s, F32) for s in shapes],
        in_specs=[VMEM] * len(operands),
        out_specs=[VMEM] * len(shapes),
        compiler_params=PARAMS,
    )(*operands)
    return out[0] if len(shapes) == 1 else out


def to_next_chip(block):
    n = lax.axis_size("cols")
    return lax.ppermute(block, "cols", [((i - 2) % n, i) for i in range(n)])


def hop(message):
    m, n = lax.axis_size("rows"), lax.axis_size("cols")
    route = [((i + m // 2) % m * n + (j - 2) % n, i * n + j) for i in range(m) for j in range(n)]
    return lax.ppermute(message, ("rows", "cols"), route)


def core_swap(block):
    n = lax.axis_size("cols")
    return lax.ppermute(block, "cols", [(i ^ 1, i) for i in range(n)])


def y_sum(part):
    n = lax.axis_size("rows")
    inner = n // 2
    terms = [part]
    for d in range(1, inner):
        route = [(i, i - i % inner + (i + d) % inner) for i in range(n)]
        terms.append(lax.ppermute(part, "rows", route))
    while len(terms) > 2:
        terms = [terms[0] + terms[1], *terms[2:]]
    return terms


def x_sum(part):
    n = lax.axis_size("rows")
    return [part, lax.ppermute(part, "rows", [(i, (i + n // 2) % n) for i in range(n)])]


def on_device(snapshots):
    w = BLK
    chips = lax.axis_size("cols") // 2
    core = lax.axis_index("cols") % 2
    rows = snapshots.shape[0] // 2
    own = lax.dynamic_slice(snapshots, (core * rows, 0), (rows, 2 * w))
    other = core_swap(lax.dynamic_slice(snapshots, ((1 - core) * rows, 0), (rows, 2 * w)))
    even, odd = jnp.where(core == 0, own, other), jnp.where(core == 0, other, own)
    top = jnp.concatenate([even[:, :w], odd[:, :w]], axis=1)
    bottom = jnp.concatenate([even[:, w:], odd[:, w:]], axis=1)

    block, small = top.shape, (2 * w, 2 * w)
    tall, taller, longer = (4 * w, 2 * w), (6 * w, 2 * w), (rows + 4 * w, 2 * w)
    part = call(first_gram_kernel, [taller], top, bottom)
    part = sum(x_sum(part + core_swap(part)))
    part, top, bottom = lax.optimization_barrier((part, top, bottom))
    left, left_bottom = to_next_chip(top), to_next_chip(bottom)
    sums = y_sum(part)
    for r in range(chips):
        if r == 0:
            urgent, message, tops = call(first_wave_kernel, [taller, tall, small], *sums)
        elif r + 1 < chips:
            urgent, message, tops = call(wave_kernel, [taller, tall, small], *sums, tops, first)
        else:
            urgent, message = call(last_wave_kernel, [tall, tall], *sums, tops, first)
        first = hop(urgent)
        top = call(side_kernel, [block], message, top, bottom)
        if r + 1 < chips:
            bottom, part = call(bottom_kernel, [longer, small], first, message, left, left_bottom, top)
            part = sum(x_sum(part + core_swap(part)))
            part, bottom = lax.optimization_barrier((part, bottom))
            soon = to_next_chip(bottom)
            sums = y_sum(part)
            left = call(side_kernel, [block], soon, left, left_bottom)
            left_bottom = soon
        else:
            bottom = call(side_kernel, [block], first, left, left_bottom)

    even = jnp.concatenate([top[:, :w], bottom[:, :w]], axis=1)
    odd = jnp.concatenate([top[:, w:], bottom[:, w:]], axis=1)
    own, other = jnp.where(core == 0, even, odd), core_swap(jnp.where(core == 0, odd, even))
    return jnp.concatenate([jnp.where(core == 0, own, other), jnp.where(core == 0, other, own)], axis=0)


def solution(mesh):
    return jax.shard_map(
        on_device, mesh=mesh, in_specs=(P("rows", "cols"),), out_specs=P("rows", "cols"), check_vma=False
    )
```

time: 1630 us -> 388 us (0.24)
  the two profiles are of different devices: /device:TPU:0 before, /device:TPU:1 now
where the time goes in v2:
time: 388 us; the launch traced here: 380 us
  waiting for transfers between devices  176 us (45%)
  Pallas kernels  124 us (32%)
  starting transfers between devices  71.3 us (18%)
    pallas_call x32, Pallas kernels, call(): pl.pallas_call(kernel, out_shape=[jax.ShapeDtypeStruct(s, F32) for s in s...  124 us
    ppermute x8, waiting for transfers between devices, hop(): return lax.ppermute(message, ('rows', 'cols'), route)  62.5 us
    ppermute x9, waiting for transfers between devices, to_next_chip(): return lax.ppermute(block, 'cols', [((i - 2) % n, i) for i in range(n)])  57.1 us
    ppermute x24, starting transfers between devices, y_sum(): terms.append(lax.ppermute(part, 'rows', route))  45.3 us
    ppermute x8, waiting for transfers between devices, x_sum(): lax.ppermute(part, 'rows', [(i, (i + n // 2) % n) for i in range(n)])  24.4 us
    ppermute x24, waiting for transfers between devices, y_sum(): terms.append(lax.ppermute(part, 'rows', route))  20.2 us
    ppermute x10, waiting for transfers between devices, core_swap(): return lax.ppermute(block, 'cols', [(i ^ 1, i) for i in range(n)])  12.2 us
    ppermute x8, starting transfers between devices, hop(): return lax.ppermute(message, ('rows', 'cols'), route)  10.4 us
  transfers between devices with their start and end apart: 59, of which 42 were waited for; matrix products, arithmetic and copies ran while one was open for 0% of the time, Pallas kernels for 27%

profile of v2, /device:TPU:1, one launch (start us, length us, event | category | flops | bytes accessed | tf_op | source)
XLA Modules:
  0.0 380.3 jit_solution(17099332142860663191)
XLA Ops:
  0.0 2.4 constant_dynamic-slice_fusion
  3.8 2.5 collective-permute-done
  11.8 4.8 %collective-permute-done.2 = f32[384,128]{1,0:T(8,128)S(1)} collective-permute-done((f32[384,128]{1,0:T(8,128)S(1)}, f32[384,128]{1,0:T(8,128)S(1)}, u32[]{:S(2)}, u32[]{:S(2)}) %collective-permute-start.2) | collective-permute-done | bytes 196640 | tf_op jit(solution)/shard_map/ppermute | solution.py:251
  16.6 2.9 collective-permute-start.7
  21.1 2.9 collective-permute-start.4
  24.4 2.3 collective-permute-start.5
  27.4 5.4 %collective-permute-done.3 = f32[384,128]{1,0:T(8,128)S(1)} collective-permute-done((f32[384,128]{1,0:T(8,128)S(1)}, f32[384,128]{1,0:T(8,128)S(1)}, u32[]{:S(2)}, u32[]{:S(2)}) %collective-permute-start.3) | collective-permute-done | bytes 196640 | tf_op jit(solution)/shard_map/ppermute | solution.py:243
  32.8 8.2 %shard_map.18 = (f32[384,128]{1,0:T(8,128)S(1)}, f32[256,128]{1,0:T(8,128)S(1)}, f32[128,128]{1,0:T(8,128)S(1)}) custom-call(f32[384,128]{1,0:T(8,128)S(1)} %add_add_fusion.near_ref, f32[384,128]{1,0:T(8,128)S(1)} %collective-permute-done.5.far_ref), custom_call_target="tpu_custom_call" | custom-call | tf_op jit(solution)/shard_map/pallas_call | solution.py:211
  41.1 3.1 collective-permute-start.6
  45.2 28.2 %collective-permute-done.6.weights_ref.old_urgent_ref = f32[384,128]{1,0:T(8,128)S(1)} collective-permute-done((f32[384,128]{1,0:T(8,128)S(1)}, f32[384,128]{1,0:T(8,128)S(1)}, u32[]{:S(2)}, u32[]{:S(2)}) %collective-permute-start.6) | collective-permute-done | bytes 196640 | tf_op jit(solution)/shard_map/ppermute | solution.py:229
  73.3 2.5 shard_map.20
  77.7 2.8 collective-permute-done.10
  80.6 3.0 collective-permute-start.12
  84.0 2.3 collective-permute-start.13
  86.3 2.0 collective-permute-done.11
  88.3 12.2 %shard_map.21 = (f32[384,128]{1,0:T(8,128)S(1)}, f32[256,128]{1,0:T(8,128)S(1)}, f32[128,128]{1,0:T(8,128)S(1)}) custom-call(f32[128,128]{1,0:T(8,128)S(1)} %add_add_fusion.7.near_ref, f32[128,128]{1,0:T(8,128)S(1)} %collective-permute-done.13.far_ref, f32[128,128]{1,0:T(8,128)S(1)} %get-tuple-element.67.old_tops_ref, ...), custom_call_target="tpu_custom_call" | custom-call | tf_op jit(solution)/shard_map/pallas_call | solution.py:211
  100.5 3.2 collective-permute-start.14
  104.7 5.5 %collective-permute-done.15.weights_ref.bottom_ref = f32[2304,128]{1,0:T(8,128)S(1)} collective-permute-done((f32[2304,128]{1,0:T(8,128)S(1)}, f32[2304,128]{1,0:T(8,128)S(1)}, u32[]{:S(2)}, u32[]{:S(2)}) %collective-permute-start.15) | collective-permute-done | bytes 1179680 | tf_op jit(solution)/shard_map/ppermute | solution.py:223
  111.2 5.1 %collective-permute-done.14.weights_ref.old_urgent_ref = f32[384,128]{1,0:T(8,128)S(1)} collective-permute-done((f32[384,128]{1,0:T(8,128)S(1)}, f32[384,128]{1,0:T(8,128)S(1)}, u32[]{:S(2)}, u32[]{:S(2)}) %collective-permute-start.14) | collective-permute-done | bytes 196640 | tf_op jit(solution)/shard_map/ppermute | solution.py:229
  116.3 2.5 shard_map.24
  120.7 2.8 collective-permute-done.17
  123.6 3.0 collective-permute-start.19
  127.0 2.3 collective-permute-start.20
  129.3 2.0 collective-permute-done.18
  131.4 12.2 %shard_map.25 = (f32[384,128]{1,0:T(8,128)S(1)}, f32[256,128]{1,0:T(8,128)S(1)}, f32[128,128]{1,0:T(8,128)S(1)}) custom-call(f32[128,128]{1,0:T(8,128)S(1)} %add_add_fusion.6.near_ref, f32[128,128]{1,0:T(8,128)S(1)} %collective-permute-done.20.far_ref, f32[128,128]{1,0:T(8,128)S(1)} %get-tuple-element.74.old_tops_ref, ...), custom_call_target="tpu_custom_call" | custom-call | tf_op jit(solution)/shard_map/pallas_call | solution.py:211
  146.5 6.7 %collective-permute-done.22.weights_ref.bottom_ref = f32[2304,128]{1,0:T(8,128)S(1)} collective-permute-done((f32[2304,128]{1,0:T(8,128)S(1)}, f32[2304,128]{1,0:T(8,128)S(1)}, u32[]{:S(2)}, u32[]{:S(2)}) %collective-permute-start.22) | collective-permute-done | bytes 1179680 | tf_op jit(solution)/shard_map/ppermute | solution.py:223
  154.2 5.1 %collective-permute-done.21.weights_ref.old_urgent_ref = f32[384,128]{1,0:T(8,128)S(1)} collective-permute-done((f32[384,128]{1,0:T(8,128)S(1)}, f32[384,128]{1,0:T(8,128)S(1)}, u32[]{:S(2)}, u32[]{:S(2)}) %collective-permute-start.21) | collective-permute-done | bytes 196640 | tf_op jit(solution)/shard_map/ppermute | solution.py:229
  159.3 2.5 shard_map.28
  163.7 2.8 collective-permute-done.24
  166.6 3.0 collective-permute-start.26
  170.0 2.3 collective-permute-start.27
  174.4 12.2 %shard_map.29 = (f32[384,128]{1,0:T(8,128)S(1)}, f32[256,128]{1,0:T(8,128)S(1)}, f32[128,128]{1,0:T(8,128)S(1)}) custom-call(f32[128,128]{1,0:T(8,128)S(1)} %add_add_fusion.5.near_ref, f32[128,128]{1,0:T(8,128)S(1)} %collective-permute-done.27.far_ref, f32[128,128]{1,0:T(8,128)S(1)} %get-tuple-element.81.old_tops_ref, ...), custom_call_target="tpu_custom_call" | custom-call | tf_op jit(solution)/shard_map/pallas_call | solution.py:211
  188.5 7.7 %collective-permute-done.29.weights_ref.bottom_ref = f32[2304,128]{1,0:T(8,128)S(1)} collective-permute-done((f32[2304,128]{1,0:T(8,128)S(1)}, f32[2304,128]{1,0:T(8,128)S(1)}, u32[]{:S(2)}, u32[]{:S(2)}) %collective-permute-start.29) | collective-permute-done | bytes 1179680 | tf_op jit(solution)/shard_map/ppermute | solution.py:223
  197.2 5.1 %collective-permute-done.28.weights_ref.old_urgent_ref = f32[384,128]{1,0:T(8,128)S(1)} collective-permute-done((f32[384,128]{1,0:T(8,128)S(1)}, f32[384,128]{1,0:T(8,128)S(1)}, u32[]{:S(2)}, u32[]{:S(2)}) %collective-permute-start.28) | collective-permute-done | bytes 196640 | tf_op jit(solution)/shard_map/ppermute | solution.py:229
  202.3 2.5 shard_map.32
  206.7 2.8 collective-permute-done.31
  209.6 3.0 collective-permute-start.33
  213.0 2.3 collective-permute-start.34
  215.3 2.0 collective-permute-done.32
  217.4 12.2 %shard_map.33 = (f32[384,128]{1,0:T(8,128)S(1)}, f32[256,128]{1,0:T(8,128)S(1)}, f32[128,128]{1,0:T(8,128)S(1)}) custom-call(f32[128,128]{1,0:T(8,128)S(1)} %add_add_fusion.4.near_ref, f32[128,128]{1,0:T(8,128)S(1)} %collective-permute-done.34.far_ref, f32[128,128]{1,0:T(8,128)S(1)} %get-tuple-element.88.old_tops_ref, ...), custom_call_target="tpu_custom_call" | custom-call | tf_op jit(solution)/shard_map/pallas_call | solution.py:211
  230.8 8.5 %collective-permute-done.36.weights_ref.bottom_ref = f32[2304,128]{1,0:T(8,128)S(1)} collective-permute-done((f32[2304,128]{1,0:T(8,128)S(1)}, f32[2304,128]{1,0:T(8,128)S(1)}, u32[]{:S(2)}, u32[]{:S(2)}) %collective-permute-start.36) | collective-permute-done | bytes 1179680 | tf_op jit(solution)/shard_map/ppermute | solution.py:223
  240.2 5.1 %collective-permute-done.35.weights_ref.old_urgent_ref = f32[384,128]{1,0:T(8,128)S(1)} collective-permute-done((f32[384,128]{1,0:T(8,128)S(1)}, f32[384,128]{1,0:T(8,128)S(1)}, u32[]{:S(2)}, u32[]{:S(2)}) %collective-permute-start.35) | collective-permute-done | bytes 196640 | tf_op jit(solution)/shard_map/ppermute | solution.py:229
  245.3 2.5 shard_map.36
  249.8 2.8 collective-permute-done.38
  252.6 3.0 collective-permute-start.40
  256.0 2.3 collective-permute-start.41
  260.4 12.2 %shard_map.37 = (f32[384,128]{1,0:T(8,128)S(1)}, f32[256,128]{1,0:T(8,128)S(1)}, f32[128,128]{1,0:T(8,128)S(1)}) custom-call(f32[128,128]{1,0:T(8,128)S(1)} %add_add_fusion.3.near_ref, f32[128,128]{1,0:T(8,128)S(1)} %collective-permute-done.41.far_ref, f32[128,128]{1,0:T(8,128)S(1)} %get-tuple-element.95.old_tops_ref, ...), custom_call_target="tpu_custom_call" | custom-call | tf_op jit(solution)/shard_map/pallas_call | solution.py:211
  273.9 8.4 %collective-permute-done.43.weights_ref.bottom_ref = f32[2304,128]{1,0:T(8,128)S(1)} collective-permute-done((f32[2304,128]{1,0:T(8,128)S(1)}, f32[2304,128]{1,0:T(8,128)S(1)}, u32[]{:S(2)}, u32[]{:S(2)}) %collective-permute-start.43) | collective-permute-done | bytes 1179680 | tf_op jit(solution)/shard_map/ppermute | solution.py:223
  283.2 5.1 %collective-permute-done.42.weights_ref.old_urgent_ref = f32[384,128]{1,0:T(8,128)S(1)} collective-permute-done((f32[384,128]{1,0:T(8,128)S(1)}, f32[384,128]{1,0:T(8,128)S(1)}, u32[]{:S(2)}, u32[]{:S(2)}) %collective-permute-start.42) | collective-permute-done | bytes 196640 | tf_op jit(solution)/shard_map/ppermute | solution.py:229
  288.4 2.5 shard_map.40
  292.8 2.8 collective-permute-done.45
  295.7 3.0 collective-permute-start.47
  299.1 2.3 collective-permute-start.48
  303.4 12.2 %shard_map.41 = (f32[384,128]{1,0:T(8,128)S(1)}, f32[256,128]{1,0:T(8,128)S(1)}, f32[128,128]{1,0:T(8,128)S(1)}) custom-call(f32[128,128]{1,0:T(8,128)S(1)} %add_add_fusion.2.near_ref, f32[128,128]{1,0:T(8,128)S(1)} %collective-permute-done.48.far_ref, f32[128,128]{1,0:T(8,128)S(1)} %get-tuple-element.102.old_tops_ref, ...), custom_call_target="tpu_custom_call" | custom-call | tf_op jit(solution)/shard_map/pallas_call | solution.py:211
  316.9 8.3 %collective-permute-done.50.weights_ref.bottom_ref = f32[2304,128]{1,0:T(8,128)S(1)} collective-permute-done((f32[2304,128]{1,0:T(8,128)S(1)}, f32[2304,128]{1,0:T(8,128)S(1)}, u32[]{:S(2)}, u32[]{:S(2)}) %collective-permute-start.50) | collective-permute-done | bytes 1179680 | tf_op jit(solution)/shard_map/ppermute | solution.py:223
  326.3 5.1 %collective-permute-done.49.weights_ref.old_urgent_ref = f32[384,128]{1,0:T(8,128)S(1)} collective-permute-done((f32[384,128]{1,0:T(8,128)S(1)}, f32[384,128]{1,0:T(8,128)S(1)}, u32[]{:S(2)}, u32[]{:S(2)}) %collective-permute-start.49) | collective-permute-done | bytes 196640 | tf_op jit(solution)/shard_map/ppermute | solution.py:229
  331.4 2.5 shard_map.44
  335.8 2.8 collective-permute-done.52
  338.7 3.0 collective-permute-start.54
  342.1 2.3 collective-permute-start.55
  346.4 8.1 %shard_map.45 = (f32[256,128]{1,0:T(8,128)S(1)}, f32[256,128]{1,0:T(8,128)S(1)}) custom-call(f32[128,128]{1,0:T(8,128)S(1)} %add_add_fusion.1.near_ref, f32[128,128]{1,0:T(8,128)S(1)} %collective-permute-done.55.far_ref, f32[128,128]{1,0:T(8,128)S(1)} %get-tuple-element.109.old_tops_ref, f32[384,128]{1,0:T(8,128)S(1)} %collective-permute-done.49.weights_ref.old_urgent_ref), custom_call_target="tpu_custom_call" | custom-call | tf_op jit(solution)/shard_map/pallas_call | solution.py:211
  356.2 12.0 %collective-permute-done.57.weights_ref.bottom_ref = f32[2304,128]{1,0:T(8,128)S(1)} collective-permute-done((f32[2304,128]{1,0:T(8,128)S(1)}, f32[2304,128]{1,0:T(8,128)S(1)}, u32[]{:S(2)}, u32[]{:S(2)}) %collective-permute-start.57) | collective-permute-done | bytes 1179680 | tf_op jit(solution)/shard_map/ppermute | solution.py:223
  369.3 3.7 collective-permute-done.56.weights_ref
  375.5 2.3 collective-permute-done.58
  (122 shorter events, 58.1 us)
Async XLA Ops:
  0.0 6.3 %copy-start = (f32[4096,128]{1,0:T(8,128)S(1)}, f32[4096,128]{1,0:T(8,128)}, u32[]{:S(2)}) copy-start(f32[4096,128]{1,0:T(8,128)} %param.1) | copy-start | bytes 6291460
  2.4 3.9 %collective-permute-start = (f32[2048,128]{1,0:T(8,128)}, f32[2048,128]{1,0:T(8,128)S(1)}, u32[]{:S(2)}, u32[]{:S(2)}) collective-permute-start(f32[2048,128]{1,0:T(8,128)} %constant_dynamic-slice_fusion), channel_id=1, source_target_pairs={{1,0},{0,1},{3,2},{2,3},{5,4},{4,5},{7,6},{6,7},{9,8},{8,9},{11,10... | collective-permute-start | bytes 3145736 | tf_op jit(solution)/shard_map/ppermute | solution.py:234
  8.9 1.5 collective-permute-start.1
  10.4 6.2 %collective-permute-start.2 = (f32[384,128]{1,0:T(8,128)S(1)}, f32[384,128]{1,0:T(8,128)S(1)}, u32[]{:S(2)}, u32[]{:S(2)}) collective-permute-start(f32[384,128]{1,0:T(8,128)S(1)} %add.109), channel_id=1, source_target_pairs={{0,64},{16,80},{32,96},{48,112},{64,0},{80,16},{96,32},{112,48},{1... | collective-permute-start | bytes 589832 | tf_op jit(solution)/shard_map/ppermute | solution.py:251
  16.6 56.7 %collective-permute-start.7 = (f32[2048,128]{1,0:T(8,128)S(1)}, f32[2048,128]{1,0:T(8,128)S(1)}, u32[]{:S(2)}, u32[]{:S(2)}) collective-permute-start(f32[2048,128]{1,0:T(8,128)S(1)} %pad_maximum_fusion.1.top_ref), channel_id=1, source_target_pairs={{14,0},{15,1},{0,2},{1,3},{2,4},{3,5},{4,6},{5,7},{6,8},{7,9},{8,1... | collective-permute-start | bytes 3145736 | tf_op jit(solution)/shard_map/ppermute | solution.py:223
  19.5 53.8 %collective-permute-start.8 = (f32[2048,128]{1,0:T(8,128)S(1)}, f32[2048,128]{1,0:T(8,128)S(1)}, u32[]{:S(2)}, u32[]{:S(2)}) collective-permute-start(f32[2048,128]{1,0:T(8,128)S(1)} %pad_maximum_fusion.2.bottom_ref), channel_id=1, source_target_pairs={{14,0},{15,1},{0,2},{1,3},{2,4},{3,5},{4,6},{5,7},{6,8},{7,9},{8,1... | collective-permute-start | bytes 3145736 | tf_op jit(solution)/shard_map/ppermute | solution.py:223
  21.1 6.3 %collective-permute-start.4 = (f32[384,128]{1,0:T(8,128)S(1)}, f32[384,128]{1,0:T(8,128)S(1)}, u32[]{:S(2)}, u32[]{:S(2)}) collective-permute-start(f32[384,128]{1,0:T(8,128)S(1)} %add.110), channel_id=1, source_target_pairs={{0,32},{16,48},{32,0},{48,16},{64,96},{80,112},{96,64},{112,80},{1... | collective-permute-start | bytes 589832 | tf_op jit(solution)/shard_map/ppermute | solution.py:243
  24.0 8.7 %collective-permute-start.3 = (f32[384,128]{1,0:T(8,128)S(1)}, f32[384,128]{1,0:T(8,128)S(1)}, u32[]{:S(2)}, u32[]{:S(2)}) collective-permute-start(f32[384,128]{1,0:T(8,128)S(1)} %add.110), channel_id=1, source_target_pairs={{0,16},{16,32},{32,48},{48,0},{64,80},{80,96},{96,112},{112,64},{1... | collective-permute-start | bytes 589832 | tf_op jit(solution)/shard_map/ppermute | solution.py:243
  24.4 8.4 %collective-permute-start.5 = (f32[384,128]{1,0:T(8,128)S(1)}, f32[384,128]{1,0:T(8,128)S(1)}, u32[]{:S(2)}, u32[]{:S(2)}) collective-permute-start(f32[384,128]{1,0:T(8,128)S(1)} %add.110), channel_id=1, source_target_pairs={{0,48},{16,0},{32,16},{48,32},{64,112},{80,64},{96,80},{112,96},{1... | collective-permute-start | bytes 589832 | tf_op jit(solution)/shard_map/ppermute | solution.py:243
  41.1 32.2 %collective-permute-start.6 = (f32[384,128]{1,0:T(8,128)S(1)}, f32[384,128]{1,0:T(8,128)S(1)}, u32[]{:S(2)}, u32[]{:S(2)}) collective-permute-start(f32[384,128]{1,0:T(8,128)S(1)} %get-tuple-element.60), channel_id=1, source_target_pairs={{78,0},{79,1},{64,2},{65,3},{66,4},{67,5},{68,6},{69,7},{70,8},{71... | collective-permute-start | bytes 589832 | tf_op jit(solution)/shard_map/ppermute | solution.py:229
  75.8 1.5 collective-permute-start.9
  77.3 3.2 collective-permute-start.10
  80.5 29.7 %collective-permute-start.15 = (f32[2304,128]{1,0:T(8,128)S(1)}, f32[2304,128]{1,0:T(8,128)S(1)}, u32[]{:S(2)}, u32[]{:S(2)}) collective-permute-start(f32[2304,128]{1,0:T(8,128)S(1)} %get-tuple-element.70.bottom_ref), channel_id=1, source_target_pairs={{14,0},{15,1},{0,2},{1,3},{2,4},{3,5},{4,6},{5,7},{6,8},{7,9},{8,1... | collective-permute-start | bytes 3538952 | tf_op jit(solution)/shard_map/ppermute | solution.py:223
  80.6 5.7 %collective-permute-start.12 = (f32[128,128]{1,0:T(8,128)S(1)}, f32[128,128]{1,0:T(8,128)S(1)}, u32[]{:S(2)}, u32[]{:S(2)}) collective-permute-start(f32[128,128]{1,0:T(8,128)S(1)} %add.114), channel_id=1, source_target_pairs={{0,32},{16,48},{32,0},{48,16},{64,96},{80,112},{96,64},{112,80},{1... | collective-permute-start | bytes 196616 | tf_op jit(solution)/shard_map/ppermute | solution.py:243
  83.6 4.7 %collective-permute-start.11 = (f32[128,128]{1,0:T(8,128)S(1)}, f32[128,128]{1,0:T(8,128)S(1)}, u32[]{:S(2)}, u32[]{:S(2)}) collective-permute-start(f32[128,128]{1,0:T(8,128)S(1)} %add.114), channel_id=1, source_target_pairs={{0,16},{16,32},{32,48},{48,0},{64,80},{80,96},{96,112},{112,64},{1... | collective-permute-start | bytes 196616 | tf_op jit(solution)/shard_map/ppermute | solution.py:243
  84.0 4.3 %collective-permute-start.13 = (f32[128,128]{1,0:T(8,128)S(1)}, f32[128,128]{1,0:T(8,128)S(1)}, u32[]{:S(2)}, u32[]{:S(2)}) collective-permute-start(f32[128,128]{1,0:T(8,128)S(1)} %add.114), channel_id=1, source_target_pairs={{0,48},{16,0},{32,16},{48,32},{64,112},{80,64},{96,80},{112,96},{1... | collective-permute-start | bytes 196616 | tf_op jit(solution)/shard_map/ppermute | solution.py:243
  100.5 15.8 %collective-permute-start.14 = (f32[384,128]{1,0:T(8,128)S(1)}, f32[384,128]{1,0:T(8,128)S(1)}, u32[]{:S(2)}, u32[]{:S(2)}) collective-permute-start(f32[384,128]{1,0:T(8,128)S(1)} %get-tuple-element.68), channel_id=1, source_target_pairs={{78,0},{79,1},{64,2},{65,3},{66,4},{67,5},{68,6},{69,7},{70,8},{71... | collective-permute-start | bytes 589832 | tf_op jit(solution)/shard_map/ppermute | solution.py:229
  118.9 1.5 collective-permute-start.16
  120.3 3.2 collective-permute-start.17
  123.5 29.7 %collective-permute-start.22 = (f32[2304,128]{1,0:T(8,128)S(1)}, f32[2304,128]{1,0:T(8,128)S(1)}, u32[]{:S(2)}, u32[]{:S(2)}) collective-permute-start(f32[2304,128]{1,0:T(8,128)S(1)} %get-tuple-element.77.bottom_ref), channel_id=1, source_target_pairs={{14,0},{15,1},{0,2},{1,3},{2,4},{3,5},{4,6},{5,7},{6,8},{7,9},{8,1... | collective-permute-start | bytes 3538952 | tf_op jit(solution)/shard_map/ppermute | solution.py:223
  123.6 5.7 %collective-permute-start.19 = (f32[128,128]{1,0:T(8,128)S(1)}, f32[128,128]{1,0:T(8,128)S(1)}, u32[]{:S(2)}, u32[]{:S(2)}) collective-permute-start(f32[128,128]{1,0:T(8,128)S(1)} %add.118), channel_id=1, source_target_pairs={{0,32},{16,48},{32,0},{48,16},{64,96},{80,112},{96,64},{112,80},{1... | collective-permute-start | bytes 196616 | tf_op jit(solution)/shard_map/ppermute | solution.py:243
  126.6 4.7 %collective-permute-start.18 = (f32[128,128]{1,0:T(8,128)S(1)}, f32[128,128]{1,0:T(8,128)S(1)}, u32[]{:S(2)}, u32[]{:S(2)}) collective-permute-start(f32[128,128]{1,0:T(8,128)S(1)} %add.118), channel_id=1, source_target_pairs={{0,16},{16,32},{32,48},{48,0},{64,80},{80,96},{96,112},{112,64},{1... | collective-permute-start | bytes 196616 | tf_op jit(solution)/shard_map/ppermute | solution.py:243
  127.0 4.3 %collective-permute-start.20 = (f32[128,128]{1,0:T(8,128)S(1)}, f32[128,128]{1,0:T(8,128)S(1)}, u32[]{:S(2)}, u32[]{:S(2)}) collective-permute-start(f32[128,128]{1,0:T(8,128)S(1)} %add.118), channel_id=1, source_target_pairs={{0,48},{16,0},{32,16},{48,32},{64,112},{80,64},{96,80},{112,96},{1... | collective-permute-start | bytes 196616 | tf_op jit(solution)/shard_map/ppermute | solution.py:243
  143.6 15.8 %collective-permute-start.21 = (f32[384,128]{1,0:T(8,128)S(1)}, f32[384,128]{1,0:T(8,128)S(1)}, u32[]{:S(2)}, u32[]{:S(2)}) collective-permute-start(f32[384,128]{1,0:T(8,128)S(1)} %get-tuple-element.75), channel_id=1, source_target_pairs={{78,0},{79,1},{64,2},{65,3},{66,4},{67,5},{68,6},{69,7},{70,8},{71... | collective-permute-start | bytes 589832 | tf_op jit(solution)/shard_map/ppermute | solution.py:229
  161.9 1.5 collective-permute-start.23
  163.3 3.2 collective-permute-start.24
  166.6 29.7 %collective-permute-start.29 = (f32[2304,128]{1,0:T(8,128)S(1)}, f32[2304,128]{1,0:T(8,128)S(1)}, u32[]{:S(2)}, u32[]{:S(2)}) collective-permute-start(f32[2304,128]{1,0:T(8,128)S(1)} %get-tuple-element.84.bottom_ref), channel_id=1, source_target_pairs={{14,0},{15,1},{0,2},{1,3},{2,4},{3,5},{4,6},{5,7},{6,8},{7,9},{8,1... | collective-permute-start | bytes 3538952 | tf_op jit(solution)/shard_map/ppermute | solution.py:223
  166.6 5.7 %collective-permute-start.26 = (f32[128,128]{1,0:T(8,128)S(1)}, f32[128,128]{1,0:T(8,128)S(1)}, u32[]{:S(2)}, u32[]{:S(2)}) collective-permute-start(f32[128,128]{1,0:T(8,128)S(1)} %add.122), channel_id=1, source_target_pairs={{0,32},{16,48},{32,0},{48,16},{64,96},{80,112},{96,64},{112,80},{1... | collective-permute-start | bytes 196616 | tf_op jit(solution)/shard_map/ppermute | solution.py:243
  169.6 4.7 %collective-permute-start.25 = (f32[128,128]{1,0:T(8,128)S(1)}, f32[128,128]{1,0:T(8,128)S(1)}, u32[]{:S(2)}, u32[]{:S(2)}) collective-permute-start(f32[128,128]{1,0:T(8,128)S(1)} %add.122), channel_id=1, source_target_pairs={{0,16},{16,32},{32,48},{48,0},{64,80},{80,96},{96,112},{112,64},{1... | collective-permute-start | bytes 196616 | tf_op jit(solution)/shard_map/ppermute | solution.py:243
  170.0 4.3 %collective-permute-start.27 = (f32[128,128]{1,0:T(8,128)S(1)}, f32[128,128]{1,0:T(8,128)S(1)}, u32[]{:S(2)}, u32[]{:S(2)}) collective-permute-start(f32[128,128]{1,0:T(8,128)S(1)} %add.122), channel_id=1, source_target_pairs={{0,48},{16,0},{32,16},{48,32},{64,112},{80,64},{96,80},{112,96},{1... | collective-permute-start | bytes 196616 | tf_op jit(solution)/shard_map/ppermute | solution.py:243
  186.6 15.8 %collective-permute-start.28 = (f32[384,128]{1,0:T(8,128)S(1)}, f32[384,128]{1,0:T(8,128)S(1)}, u32[]{:S(2)}, u32[]{:S(2)}) collective-permute-start(f32[384,128]{1,0:T(8,128)S(1)} %get-tuple-element.82), channel_id=1, source_target_pairs={{78,0},{79,1},{64,2},{65,3},{66,4},{67,5},{68,6},{69,7},{70,8},{71... | collective-permute-start | bytes 589832 | tf_op jit(solution)/shard_map/ppermute | solution.py:229
  204.9 1.5 collective-permute-start.30
  206.4 3.2 collective-permute-start.31
  209.6 29.7 %collective-permute-start.36 = (f32[2304,128]{1,0:T(8,128)S(1)}, f32[2304,128]{1,0:T(8,128)S(1)}, u32[]{:S(2)}, u32[]{:S(2)}) collective-permute-start(f32[2304,128]{1,0:T(8,128)S(1)} %get-tuple-element.91.bottom_ref), channel_id=1, source_target_pairs={{14,0},{15,1},{0,2},{1,3},{2,4},{3,5},{4,6},{5,7},{6,8},{7,9},{8,1... | collective-permute-start | bytes 3538952 | tf_op jit(solution)/shard_map/ppermute | solution.py:223
  209.6 5.7 %collective-permute-start.33 = (f32[128,128]{1,0:T(8,128)S(1)}, f32[128,128]{1,0:T(8,128)S(1)}, u32[]{:S(2)}, u32[]{:S(2)}) collective-permute-start(f32[128,128]{1,0:T(8,128)S(1)} %add.126), channel_id=1, source_target_pairs={{0,32},{16,48},{32,0},{48,16},{64,96},{80,112},{96,64},{112,80},{1... | collective-permute-start | bytes 196616 | tf_op jit(solution)/shard_map/ppermute | solution.py:243
  212.6 4.7 %collective-permute-start.32 = (f32[128,128]{1,0:T(8,128)S(1)}, f32[128,128]{1,0:T(8,128)S(1)}, u32[]{:S(2)}, u32[]{:S(2)}) collective-permute-start(f32[128,128]{1,0:T(8,128)S(1)} %add.126), channel_id=1, source_target_pairs={{0,16},{16,32},{32,48},{48,0},{64,80},{80,96},{96,112},{112,64},{1... | collective-permute-start | bytes 196616 | tf_op jit(solution)/shard_map/ppermute | solution.py:243
  213.0 4.3 %collective-permute-start.34 = (f32[128,128]{1,0:T(8,128)S(1)}, f32[128,128]{1,0:T(8,128)S(1)}, u32[]{:S(2)}, u32[]{:S(2)}) collective-permute-start(f32[128,128]{1,0:T(8,128)S(1)} %add.126), channel_id=1, source_target_pairs={{0,48},{16,0},{32,16},{48,32},{64,112},{80,64},{96,80},{112,96},{1... | collective-permute-start | bytes 196616 | tf_op jit(solution)/shard_map/ppermute | solution.py:243
  229.6 15.8 %collective-permute-start.35 = (f32[384,128]{1,0:T(8,128)S(1)}, f32[384,128]{1,0:T(8,128)S(1)}, u32[]{:S(2)}, u32[]{:S(2)}) collective-permute-start(f32[384,128]{1,0:T(8,128)S(1)} %get-tuple-element.89), channel_id=1, source_target_pairs={{78,0},{79,1},{64,2},{65,3},{66,4},{67,5},{68,6},{69,7},{70,8},{71... | collective-permute-start | bytes 589832 | tf_op jit(solution)/shard_map/ppermute | solution.py:229
  247.9 1.5 collective-permute-start.37
  249.4 3.2 collective-permute-start.38
  252.6 29.7 %collective-permute-start.43 = (f32[2304,128]{1,0:T(8,128)S(1)}, f32[2304,128]{1,0:T(8,128)S(1)}, u32[]{:S(2)}, u32[]{:S(2)}) collective-permute-start(f32[2304,128]{1,0:T(8,128)S(1)} %get-tuple-element.98.bottom_ref), channel_id=1, source_target_pairs={{14,0},{15,1},{0,2},{1,3},{2,4},{3,5},{4,6},{5,7},{6,8},{7,9},{8,1... | collective-permute-start | bytes 3538952 | tf_op jit(solution)/shard_map/ppermute | solution.py:223
  252.6 5.7 %collective-permute-start.40 = (f32[128,128]{1,0:T(8,128)S(1)}, f32[128,128]{1,0:T(8,128)S(1)}, u32[]{:S(2)}, u32[]{:S(2)}) collective-permute-start(f32[128,128]{1,0:T(8,128)S(1)} %add.130), channel_id=1, source_target_pairs={{0,32},{16,48},{32,0},{48,16},{64,96},{80,112},{96,64},{112,80},{1... | collective-permute-start | bytes 196616 | tf_op jit(solution)/shard_map/ppermute | solution.py:243
  255.7 4.7 %collective-permute-start.39 = (f32[128,128]{1,0:T(8,128)S(1)}, f32[128,128]{1,0:T(8,128)S(1)}, u32[]{:S(2)}, u32[]{:S(2)}) collective-permute-start(f32[128,128]{1,0:T(8,128)S(1)} %add.130), channel_id=1, source_target_pairs={{0,16},{16,32},{32,48},{48,0},{64,80},{80,96},{96,112},{112,64},{1... | collective-permute-start | bytes 196616 | tf_op jit(solution)/shard_map/ppermute | solution.py:243
  256.0 4.3 %collective-permute-start.41 = (f32[128,128]{1,0:T(8,128)S(1)}, f32[128,128]{1,0:T(8,128)S(1)}, u32[]{:S(2)}, u32[]{:S(2)}) collective-permute-start(f32[128,128]{1,0:T(8,128)S(1)} %add.130), channel_id=1, source_target_pairs={{0,48},{16,0},{32,16},{48,32},{64,112},{80,64},{96,80},{112,96},{1... | collective-permute-start | bytes 196616 | tf_op jit(solution)/shard_map/ppermute | solution.py:243
  272.6 15.8 %collective-permute-start.42 = (f32[384,128]{1,0:T(8,128)S(1)}, f32[384,128]{1,0:T(8,128)S(1)}, u32[]{:S(2)}, u32[]{:S(2)}) collective-permute-start(f32[384,128]{1,0:T(8,128)S(1)} %get-tuple-element.96), channel_id=1, source_target_pairs={{78,0},{79,1},{64,2},{65,3},{66,4},{67,5},{68,6},{69,7},{70,8},{71... | collective-permute-start | bytes 589832 | tf_op jit(solution)/shard_map/ppermute | solution.py:229
  290.9 1.5 collective-permute-start.44
  292.4 3.2 collective-permute-start.45
  295.6 29.7 %collective-permute-start.50 = (f32[2304,128]{1,0:T(8,128)S(1)}, f32[2304,128]{1,0:T(8,128)S(1)}, u32[]{:S(2)}, u32[]{:S(2)}) collective-permute-start(f32[2304,128]{1,0:T(8,128)S(1)} %get-tuple-element.105.bottom_ref), channel_id=1, source_target_pairs={{14,0},{15,1},{0,2},{1,3},{2,4},{3,5},{4,6},{5,7},{6,8},{7,9},{8,1... | collective-permute-start | bytes 3538952 | tf_op jit(solution)/shard_map/ppermute | solution.py:223
  295.7 5.7 %collective-permute-start.47 = (f32[128,128]{1,0:T(8,128)S(1)}, f32[128,128]{1,0:T(8,128)S(1)}, u32[]{:S(2)}, u32[]{:S(2)}) collective-permute-start(f32[128,128]{1,0:T(8,128)S(1)} %add.134), channel_id=1, source_target_pairs={{0,32},{16,48},{32,0},{48,16},{64,96},{80,112},{96,64},{112,80},{1... | collective-permute-start | bytes 196616 | tf_op jit(solution)/shard_map/ppermute | solution.py:243
  298.7 4.7 %collective-permute-start.46 = (f32[128,128]{1,0:T(8,128)S(1)}, f32[128,128]{1,0:T(8,128)S(1)}, u32[]{:S(2)}, u32[]{:S(2)}) collective-permute-start(f32[128,128]{1,0:T(8,128)S(1)} %add.134), channel_id=1, source_target_pairs={{0,16},{16,32},{32,48},{48,0},{64,80},{80,96},{96,112},{112,64},{1... | collective-permute-start | bytes 196616 | tf_op jit(solution)/shard_map/ppermute | solution.py:243
  299.1 4.3 %collective-permute-start.48 = (f32[128,128]{1,0:T(8,128)S(1)}, f32[128,128]{1,0:T(8,128)S(1)}, u32[]{:S(2)}, u32[]{:S(2)}) collective-permute-start(f32[128,128]{1,0:T(8,128)S(1)} %add.134), channel_id=1, source_target_pairs={{0,48},{16,0},{32,16},{48,32},{64,112},{80,64},{96,80},{112,96},{1... | collective-permute-start | bytes 196616 | tf_op jit(solution)/shard_map/ppermute | solution.py:243
  315.6 15.8 %collective-permute-start.49 = (f32[384,128]{1,0:T(8,128)S(1)}, f32[384,128]{1,0:T(8,128)S(1)}, u32[]{:S(2)}, u32[]{:S(2)}) collective-permute-start(f32[384,128]{1,0:T(8,128)S(1)} %get-tuple-element.103), channel_id=1, source_target_pairs={{78,0},{79,1},{64,2},{65,3},{66,4},{67,5},{68,6},{69,7},{70,8},{71... | collective-permute-start | bytes 589832 | tf_op jit(solution)/shard_map/ppermute | solution.py:229
  333.9 1.5 collective-permute-start.51
  335.4 3.2 collective-permute-start.52
  338.6 29.7 %collective-permute-start.57 = (f32[2304,128]{1,0:T(8,128)S(1)}, f32[2304,128]{1,0:T(8,128)S(1)}, u32[]{:S(2)}, u32[]{:S(2)}) collective-permute-start(f32[2304,128]{1,0:T(8,128)S(1)} %get-tuple-element.111.bottom_ref), channel_id=1, source_target_pairs={{14,0},{15,1},{0,2},{1,3},{2,4},{3,5},{4,6},{5,7},{6,8},{7,9},{8,1... | collective-permute-start | bytes 3538952 | tf_op jit(solution)/shard_map/ppermute | solution.py:223
  338.7 5.7 %collective-permute-start.54 = (f32[128,128]{1,0:T(8,128)S(1)}, f32[128,128]{1,0:T(8,128)S(1)}, u32[]{:S(2)}, u32[]{:S(2)}) collective-permute-start(f32[128,128]{1,0:T(8,128)S(1)} %add.138), channel_id=1, source_target_pairs={{0,32},{16,48},{32,0},{48,16},{64,96},{80,112},{96,64},{112,80},{1... | collective-permute-start | bytes 196616 | tf_op jit(solution)/shard_map/ppermute | solution.py:243
  341.7 4.7 %collective-permute-start.53 = (f32[128,128]{1,0:T(8,128)S(1)}, f32[128,128]{1,0:T(8,128)S(1)}, u32[]{:S(2)}, u32[]{:S(2)}) collective-permute-start(f32[128,128]{1,0:T(8,128)S(1)} %add.138), channel_id=1, source_target_pairs={{0,16},{16,32},{32,48},{48,0},{64,80},{80,96},{96,112},{112,64},{1... | collective-permute-start | bytes 196616 | tf_op jit(solution)/shard_map/ppermute | solution.py:243
  342.1 4.3 %collective-permute-start.55 = (f32[128,128]{1,0:T(8,128)S(1)}, f32[128,128]{1,0:T(8,128)S(1)}, u32[]{:S(2)}, u32[]{:S(2)}) collective-permute-start(f32[128,128]{1,0:T(8,128)S(1)} %add.138), channel_id=1, source_target_pairs={{0,48},{16,0},{32,16},{48,32},{64,112},{80,64},{96,80},{112,96},{1... | collective-permute-start | bytes 196616 | tf_op jit(solution)/shard_map/ppermute | solution.py:243
  355.5 17.4 %collective-permute-start.56 = (f32[256,128]{1,0:T(8,128)S(1)}, f32[256,128]{1,0:T(8,128)S(1)}, u32[]{:S(2)}, u32[]{:S(2)}) collective-permute-start(f32[256,128]{1,0:T(8,128)S(1)} %get-tuple-element.112), channel_id=1, source_target_pairs={{78,0},{79,1},{64,2},{65,3},{66,4},{67,5},{68,6},{69,7},{70,8},{71... | collective-permute-start | bytes 393224 | tf_op jit(solution)/shard_map/ppermute | solution.py:229
  374.9 2.9 collective-permute-start.58
